TPU v7x, 32 devices: a whole 2x2x4 slice. The times are simulated.
32 devices in a mesh: query: 4 (over y, x), tok: 8 (over z, core).
Axes of the slice: x: 2, y: 2, z: 4, core: 2. Of those that a mesh axis runs over, the one named last changes fastest.
Arguments:
- queries: bfloat16 [16384, 128], P('query'), may hold values from -16 to 16, as said below
- documents: bfloat16 [16384, 128], P('tok'), may hold values from -10 to 10, as said below
- cotangent: float32 [512], P('query'), may hold values from -6 to 6
Outputs:
- grad_queries: float32 [16384, 128], P(('query', 'tok'))
- grad_documents: float32 [8, 2048, 128], P('tok', 'query')
Inputs may be any that keep to these rules, and one draw needn't show every extreme that they name: `documents`: document embeddings of order one. `queries`: query embeddings of order one.
All inputs are finite; a program needn't handle non-finite values.
Results may differ from a plain program's by a relative error of at most 0.0029.
Values may be sent and summed in bfloat16 or wider, within the bound.
No kernel may reach another device: no remote copies, remote signals or barrier semaphores. Data moves between devices by JAX's collectives and lax.ppermute only.
A program may use at most 64 MiB of HBM per device.

v0:
```python
import jax
import jax.numpy as jnp
from jax import lax
from jax.sharding import PartitionSpec as P

QLEN = 32


inv_temp = 2.0


def score_rows(q_rows, doc_rows):
    return (
        lax.dot_general(
            q_rows, doc_rows, (((1,), (1,)), ((), ())), preferred_element_type=jnp.float32
        )
        * inv_temp
    )


def doc_terms(q_rows, log_rows, weight_rows, doc_rows):
    scores = score_rows(q_rows, doc_rows)
    probs = jnp.exp(scores - log_rows[:, None])
    scaled = (weight_rows[:, None] * probs).astype(jnp.bfloat16)
    return lax.dot_general(
        scaled, q_rows, (((0,), (0,)), ((), ())), preferred_element_type=jnp.float32
    )


def shards(queries, documents, cotangent):
    n_rows, feat_width = queries.shape
    n_docs = documents.shape[0]
    blk_rows = min(512, n_rows)
    n_blocks = n_rows // blk_rows
    row_weight = jnp.broadcast_to(cotangent[:, None], (cotangent.shape[0], QLEN)).reshape(-1)
    q_blocks = queries.reshape(n_blocks, blk_rows, feat_width)

    def local_stats(carry, q_rows):
        scores = score_rows(q_rows, documents)
        row_top = jnp.max(scores, axis=1)
        row_total = jnp.sum(jnp.exp(scores - row_top[:, None]), axis=1)
        return (carry, (row_top, row_total))

    _, (row_tops, row_totals) = lax.scan(local_stats, 0, q_blocks)
    row_tops = row_tops.reshape(-1)
    row_totals = row_totals.reshape(-1)
    top_all = lax.pmax(row_tops, "tok")
    total_all = lax.psum(row_totals * jnp.exp(row_tops - top_all), "tok")
    log_total = top_all + jnp.log(total_all)
    log_blocks = log_total.reshape(n_blocks, blk_rows)
    weight_blocks = row_weight.reshape(n_blocks, blk_rows)

    def backward_query(carry, inputs_blk):
        q_rows, log_rows, weight_rows = inputs_blk
        scores = score_rows(q_rows, documents)
        weights_low = jnp.exp(scores - log_rows[:, None]).astype(jnp.bfloat16)
        grad_rows = weight_rows[:, None] * jnp.dot(
            weights_low, documents, preferred_element_type=jnp.float32
        )
        return (carry, grad_rows)

    _, grad_blocks = lax.scan(backward_query, 0, (q_blocks, log_blocks, weight_blocks))
    all_logs, all_weights = (
        lax.all_gather(log_total, "query", axis=0, tiled=True),
        lax.all_gather(row_weight, "query", axis=0, tiled=True),
    )
    sub_docs = n_docs // lax.axis_size("query")
    own_docs = lax.dynamic_slice_in_dim(documents, lax.axis_index("query") * sub_docs, sub_docs, 0)
    doc_total = jnp.zeros((sub_docs, feat_width), jnp.float32)
    q_piece = lax.all_gather(queries, "query", axis=0, tiled=True)
    count = q_piece.shape[0]
    parts_n = count // 512

    def inner(total_now, inputs_blk):
        return (total_now + doc_terms(inputs_blk[0], inputs_blk[1], inputs_blk[2], own_docs), 0)

    doc_total, _ = lax.scan(
        inner,
        doc_total,
        (
            q_piece.reshape(parts_n, 512, feat_width),
            all_logs.reshape(parts_n, 512),
            all_weights.reshape(parts_n, 512),
        ),
    )
    query_terms = grad_blocks.reshape(n_rows, feat_width)
    grad_q = lax.psum_scatter(query_terms, "tok", scatter_dimension=0, tiled=True)
    return (grad_q, doc_total[None])


def solution(mesh):
    placed = (P("query", None), P("tok", None), P("query"))
    return jax.shard_map(
        shards,
        mesh=mesh,
        in_specs=placed,
        out_specs=(P(("query", "tok"), None), P("tok", "query", None)),
        check_vma=False,
    )
```

profile of v0, /device:TPU:0, one launch (start us, length us, event | category | flops | bytes accessed | tf_op | source)
XLA Modules:
  0.0 196.0 jit_solution(16010578593961780501)
XLA Ops:
  8.8 23.2 %while.33 = (s32[]{:T(128)}, f32[8,512]{1,0:T(8,128)S(1)}, f32[8,512]{1,0:T(8,128)S(1)}, bf16[8,512,128]{2,1,0:T(8,128)(2,1)}, bf16[2048,128]{1,0:T(8,128)(2,1)}, /*index=5*/s32[]{:T(128)}, s32[]{:T(128)}) while((s32[]{:T(128)}, f32[8,512]{1,0:T(8,128)S(1)}, f32[8,512]{1,0:T(8,128)S(1)}, bf16[8,512,128]{2,1,0:T(8,128)(2,1)}, ...), condition=%wide.region_3.4_spmd, body=%wide.region_0.3_spmd.sunk | while | flops 273677312 | bytes 9058901 | solution.py:44
  8.8 1.9 multiply_reduce_fusion.2
  11.7 1.9 multiply_reduce_fusion.2
  14.6 1.9 multiply_reduce_fusion.2
  17.5 1.9 multiply_reduce_fusion.2
  20.4 2.0 %multiply_reduce_fusion.2 = (f32[512]{0:T(512)S(1)}, f32[512,2048]{1,0:T(8,128)S(1)}) fusion(bf16[2048,128]{1,0:T(8,128)(2,1)} %get-tuple-element.294, bf16[8,512,128]{2,1,0:T(8,128)(2,1)} %get-tuple-element.293, s32[]{:T(128)} %get-tuple-element.283), kind=kOutput, calls=%fused_computation.1.clone.1 | convolution fusion | flops 270532096 | bytes 4852224 | tf_op jit(solution)/shard_map/while/body/eval_jaxpr/dot_general | solution.py:14
  23.4 1.9 multiply_reduce_fusion.2
  26.2 1.9 multiply_reduce_fusion.2
  29.1 1.9 multiply_reduce_fusion.2
  32.0 30.2 %pmax.7 = f32[4096]{0:T(1024)S(1)} all-reduce(f32[4096]{0:T(1024)S(1)} %bitcast.69), channel_id=1, replica_groups=mesh['query'=4,'tok'=8] {'tok'}, use_global_device_ids=true, to_apply=%region_4.5 | all-reduce | flops 4096 | bytes 32768 | tf_op jit(solution)/shard_map/pmax | solution.py:47
  62.2 25.9 %psum.7 = f32[4096]{0:T(1024)S(1)} all-reduce(f32[4096]{0:T(1024)S(1)} %exponential_multiply_fusion), channel_id=1, replica_groups=mesh['query'=4,'tok'=8] {'tok'}, use_global_device_ids=true, to_apply=%region_5.6 | all-reduce | flops 4096 | bytes 32768 | tf_op jit(solution)/shard_map/psum | solution.py:48
  88.4 26.7 %while.34 = (s32[]{:T(128)}, f32[8,512,128]{2,1,0:T(8,128)}, f32[8,512]{1,0:T(8,128)S(1)}, bf16[8,512,128]{2,1,0:T(8,128)(2,1)}, bf16[2048,128]{1,0:T(8,128)(2,1)}, /*index=5*/f32[8,512]{1,0:T(8,128)S(1)}, s32[]{:T(128)}) while((s32[]{:T(128)}, f32[8,512,128]{2,1,0:T(8,128)}, f32[8,512]{1,0:T(8,128)S(1)}, bf16[8,512,128]{2,1,0:T(8,128)(2,1)}, ...), condition=%wide.region_7.8_spmd, body=%wide.region_6.7_spmd.sunk | while | flops 540082176 | bytes 1455185 | solution.py:62
  88.5 3.3 %fusion.48 = f32[8,512,128]{2,1,0:T(8,128)} fusion(f32[8,512,128]{2,1,0:T(8,128)} %get-tuple-element.305, s32[]{:T(128)} %get-tuple-element.304, bf16[2048,128]{1,0:T(8,128)(2,1)} %get-tuple-element.315, f32[512]{0:T(512)S(1)} %bitcast.74, bf16[8,512,128]{2,1,0:T(8,128)(2,1)} %get-tuple-element.314, f32[512]{0:T(512)S(1)} %bitcast.75), kind=kOutput, calls=%fused_computation.10.clone.1 | convolution fusion | flops 540082176 | bytes 1446912 | tf_op jit(solution)/shard_map/while/body/eval_jaxpr/dot_general | solution.py:57
  91.8 3.3 %fusion.48 = f32[8,512,128]{2,1,0:T(8,128)} fusion(f32[8,512,128]{2,1,0:T(8,128)} %get-tuple-element.305, s32[]{:T(128)} %get-tuple-element.304, bf16[2048,128]{1,0:T(8,128)(2,1)} %get-tuple-element.315, f32[512]{0:T(512)S(1)} %bitcast.74, bf16[8,512,128]{2,1,0:T(8,128)(2,1)} %get-tuple-element.314, f32[512]{0:T(512)S(1)} %bitcast.75), kind=kOutput, calls=%fused_computation.10.clone.1 | convolution fusion | flops 540082176 | bytes 1446912 | tf_op jit(solution)/shard_map/while/body/eval_jaxpr/dot_general | solution.py:57
  95.1 3.3 %fusion.48 = f32[8,512,128]{2,1,0:T(8,128)} fusion(f32[8,512,128]{2,1,0:T(8,128)} %get-tuple-element.305, s32[]{:T(128)} %get-tuple-element.304, bf16[2048,128]{1,0:T(8,128)(2,1)} %get-tuple-element.315, f32[512]{0:T(512)S(1)} %bitcast.74, bf16[8,512,128]{2,1,0:T(8,128)(2,1)} %get-tuple-element.314, f32[512]{0:T(512)S(1)} %bitcast.75), kind=kOutput, calls=%fused_computation.10.clone.1 | convolution fusion | flops 540082176 | bytes 1446912 | tf_op jit(solution)/shard_map/while/body/eval_jaxpr/dot_general | solution.py:57
  98.4 3.3 %fusion.48 = f32[8,512,128]{2,1,0:T(8,128)} fusion(f32[8,512,128]{2,1,0:T(8,128)} %get-tuple-element.305, s32[]{:T(128)} %get-tuple-element.304, bf16[2048,128]{1,0:T(8,128)(2,1)} %get-tuple-element.315, f32[512]{0:T(512)S(1)} %bitcast.74, bf16[8,512,128]{2,1,0:T(8,128)(2,1)} %get-tuple-element.314, f32[512]{0:T(512)S(1)} %bitcast.75), kind=kOutput, calls=%fused_computation.10.clone.1 | convolution fusion | flops 540082176 | bytes 1446912 | tf_op jit(solution)/shard_map/while/body/eval_jaxpr/dot_general | solution.py:57
  101.8 3.3 %fusion.48 = f32[8,512,128]{2,1,0:T(8,128)} fusion(f32[8,512,128]{2,1,0:T(8,128)} %get-tuple-element.305, s32[]{:T(128)} %get-tuple-element.304, bf16[2048,128]{1,0:T(8,128)(2,1)} %get-tuple-element.315, f32[512]{0:T(512)S(1)} %bitcast.74, bf16[8,512,128]{2,1,0:T(8,128)(2,1)} %get-tuple-element.314, f32[512]{0:T(512)S(1)} %bitcast.75), kind=kOutput, calls=%fused_computation.10.clone.1 | convolution fusion | flops 540082176 | bytes 1446912 | tf_op jit(solution)/shard_map/while/body/eval_jaxpr/dot_general | solution.py:57
  105.1 3.3 %fusion.48 = f32[8,512,128]{2,1,0:T(8,128)} fusion(f32[8,512,128]{2,1,0:T(8,128)} %get-tuple-element.305, s32[]{:T(128)} %get-tuple-element.304, bf16[2048,128]{1,0:T(8,128)(2,1)} %get-tuple-element.315, f32[512]{0:T(512)S(1)} %bitcast.74, bf16[8,512,128]{2,1,0:T(8,128)(2,1)} %get-tuple-element.314, f32[512]{0:T(512)S(1)} %bitcast.75), kind=kOutput, calls=%fused_computation.10.clone.1 | convolution fusion | flops 540082176 | bytes 1446912 | tf_op jit(solution)/shard_map/while/body/eval_jaxpr/dot_general | solution.py:57
  108.5 3.3 %fusion.48 = f32[8,512,128]{2,1,0:T(8,128)} fusion(f32[8,512,128]{2,1,0:T(8,128)} %get-tuple-element.305, s32[]{:T(128)} %get-tuple-element.304, bf16[2048,128]{1,0:T(8,128)(2,1)} %get-tuple-element.315, f32[512]{0:T(512)S(1)} %bitcast.74, bf16[8,512,128]{2,1,0:T(8,128)(2,1)} %get-tuple-element.314, f32[512]{0:T(512)S(1)} %bitcast.75), kind=kOutput, calls=%fused_computation.10.clone.1 | convolution fusion | flops 540082176 | bytes 1446912 | tf_op jit(solution)/shard_map/while/body/eval_jaxpr/dot_general | solution.py:57
  111.8 3.3 %fusion.48 = f32[8,512,128]{2,1,0:T(8,128)} fusion(f32[8,512,128]{2,1,0:T(8,128)} %get-tuple-element.305, s32[]{:T(128)} %get-tuple-element.304, bf16[2048,128]{1,0:T(8,128)(2,1)} %get-tuple-element.315, f32[512]{0:T(512)S(1)} %bitcast.74, bf16[8,512,128]{2,1,0:T(8,128)(2,1)} %get-tuple-element.314, f32[512]{0:T(512)S(1)} %bitcast.75), kind=kOutput, calls=%fused_computation.10.clone.1 | convolution fusion | flops 540082176 | bytes 1446912 | tf_op jit(solution)/shard_map/while/body/eval_jaxpr/dot_general | solution.py:57
  115.2 8.2 %all_gather.11 = f32[16384]{0:T(1024)S(1)} all-gather(f32[4096]{0:T(1024)S(1)} %log_add_fusion), channel_id=1, replica_groups=mesh['query'=4,'tok'=8] {'query'}, dimensions={0}, use_global_device_ids=true | all-gather | bytes 81920 | tf_op jit(solution)/shard_map/all_gather | solution.py:64
  124.5 8.2 %all_gather.9 = f32[16384]{0:T(1024)S(1)} all-gather(f32[4096]{0:T(1024)S(1)} %reshape.49), channel_id=1, replica_groups=mesh['query'=4,'tok'=8] {'query'}, dimensions={0}, use_global_device_ids=true | all-gather | bytes 81920 | tf_op jit(solution)/shard_map/all_gather | solution.py:65
  132.8 55.1 %while.35 = (s32[]{:T(128)}, f32[512,128]{1,0:T(8,128)S(1)}, f32[32,512]{1,0:T(8,128)S(1)}, bf16[32,512,128]{2,1,0:T(8,128)(2,1)}, bf16[512,128]{1,0:T(8,128)(2,...) while((s32[]{:T(128)}, f32[512,128]{1,0:T(8,128)S(1)}, f32[32,512]{1,0:T(8,128)S(1)}, ...), condition=%wide.region_10.11_spmd.clone, body=%wide.region_9.10_spmd.clone.sunk | while | flops 135397376 | bytes 930915 | solution.py:77
  132.8 1.7 fusion.52
  138.0 1.7 fusion.52
  143.1 1.7 fusion.52
  148.3 1.7 fusion.52
  153.5 1.7 fusion.52
  158.6 1.7 fusion.52
  163.8 1.7 fusion.52
  168.9 1.7 fusion.52
  174.1 1.7 fusion.52
  (114 shorter events, 49.4 us)
Async XLA Ops:
  8.0 124.8 %all-gather.2.cloned.1.call-start = ((), (), s32[]{:S(2)}) async-start(), calls=%async_computation.2 | async-start | bytes 5242880 | tf_op jit(solution)/shard_map/all_gather | solution.py:70
  8.7 179.2 %reduce-scatter.2.cloned.1.call-start = ((), (), s32[]{:S(2)}) async-start(), calls=%async_computation.1 | async-start | bytes 2359296 | tf_op jit(solution)/shard_map/reduce_scatter | solution.py:87
  8.8 79.4 %copy-start = (f32[128]{0:T(128)S(1)}, f32[128]{0:T(128)}, u32[]{:S(2)}) copy-start(f32[128]{0:T(128)} %param.11) | copy-start | bytes 1540
  187.8 0.7 copy-start.1
Sparse Core Ops, SparseCore 0:
  10.7 55.3 all-gather.1
Sparse Core Ops, SparseCore 1:
  115.2 33.7 reduce-scatter.1
where the time goes:
time: 197 us; the launch traced here: 196 us
  matrix products  95.5 us (48%)
  blocking collectives  72.6 us (37%)
  between operations  15.6 us (8%)
  other arithmetic  6.63 us (3%)
  local copies, waits for them, and re-layouts  3.42 us (2%)
    dot_general x32, matrix products, doc_terms(): lax.dot_general(scaled, q_rows, (((0,), (0,)), ((), ())), preferred_eleme...  53.6 us
    pmax x1, blocking collectives, shards(): top_all = lax.pmax(row_tops, 'tok')  30.2 us
    dot_general x8, matrix products, backward_query(): jnp.dot(weights_low, documents, preferred_element_type=jnp.float32)  26.6 us
    psum x1, blocking collectives, shards(): total_all = lax.psum(row_totals * jnp.exp(row_tops - top_all), 'tok')  25.9 us
    dot_general x8, matrix products, score_rows(): lax.dot_general(q_rows, doc_rows, (((1,), (1,)), ((), ())), preferred_ele...  15.4 us
    all_gather x1, blocking collectives, shards(): lax.all_gather(log_total, 'query', axis=0, tiled=True)  8.24 us
    all_gather x1, blocking collectives, shards(): lax.all_gather(row_weight, 'query', axis=0, tiled=True)  8.22 us
    reduce_sum x8, other arithmetic, local_stats(): row_total = jnp.sum(jnp.exp(scores - row_top[:, None]), axis=1)  6.6 us
  transfers between devices with their start and end apart: 2, of which 0 were waited for; matrix products, arithmetic and copies ran while one was open for 54% of the time, Pallas kernels for 0%

commit v1 on v0

v1 whole, which is shorter than its diff:
```python
import functools

import jax
import jax.numpy as jnp
from jax import lax
from jax.experimental import pallas as pl
from jax.experimental.pallas import tpu as pltpu
from jax.sharding import PartitionSpec as P

QLEN = 32
SCALE = 2.0 * 1.4426950408889634
ROOM = 30.0
F32 = jnp.float32
BF16 = jnp.bfloat16


def nt_dot(a, b):
    return lax.dot_general(a, b, (((1,), (1,)), ((), ())), preferred_element_type=F32)


def nn_dot(a, b):
    return lax.dot_general(a, b, (((1,), (0,)), ((), ())), preferred_element_type=F32)


def logsum2(terms):
    top = functools.reduce(jnp.maximum, terms)
    return top + jnp.log2(sum(jnp.exp2(t - top) for t in terms))


def tile_kernel(place, q_ref, d_ref, e_ref, qt_ref, even_ref, odd_ref, lse_ref, top_ref, dt_ref, s_ref):
    nb, nd, blk = e_ref.shape
    width = d_ref.shape[1]
    step = min(256, nd)
    me = place[0]
    dt_ref[:width, :] = d_ref[...].T
    extra = (dt_ref.shape[0] - width, nd)
    dt_ref[width:, :] = jnp.where(lax.broadcasted_iota(jnp.int32, extra, 0) == 0, 1.0, 0.0).astype(BF16)

    def rows_of(p):
        return q_ref[pl.ds(pl.multiple_of((me ^ p) * blk, blk), blk), :]

    def column_max(s):
        return jnp.max(jnp.max(s.reshape(step // 8, 8, blk), axis=0), axis=0, keepdims=True)

    def finish(p, top):
        total = nn_dot(dt_ref[...], e_ref[p])
        mass = total[width : width + 1, :]
        mean = total[:width, :] * (1.0 / mass)
        half = p // 2

        @pl.when(p % 2 == 0)
        def _():
            even_ref[half] = mean

        @pl.when(p % 2 == 1)
        def _():
            odd_ref[half] = mean

        lse_ref[p] = top + jnp.log2(mass)
        top_ref[p] = top

    def quick(p, carry):
        rows = rows_of(p)
        qt_ref[p] = rows.T
        top = column_max(nt_dot(d_ref[:step, :], rows)) * SCALE
        for at in range(0, nd, step):
            s = nt_dot(d_ref[at : at + step, :], rows)
            e_ref[p, at : at + step, :] = jnp.exp2(s * SCALE - top).astype(BF16)
        finish(p, top)
        return jnp.maximum(carry, lse_ref[p] - top)

    spread = lax.fori_loop(0, nb, quick, jnp.zeros((1, blk), F32))

    @pl.when(jnp.logical_not(jnp.max(spread) <= ROOM))
    def _():
        def careful(p, carry):
            rows = rows_of(p)
            top = None
            for at in range(0, nd, step):
                s = nt_dot(d_ref[at : at + step, :], rows)
                s_ref[at : at + step, :] = s
                here = column_max(s)
                top = here if top is None else jnp.maximum(top, here)
            top = top * SCALE
            for at in range(0, nd, step):
                e_ref[p, at : at + step, :] = jnp.exp2(s_ref[at : at + step, :] * SCALE - top).astype(BF16)
            finish(p, top)
            return carry

        lax.fori_loop(0, nb, careful, 0)


def pair_kernel(even_ref, other_ref, lse_ref, other_lse_ref, pair_ref, own_ref, *send_refs):
    nb = lse_ref.shape[0]
    for p in range(nb):
        mine, theirs = lse_ref[p], other_lse_ref[p ^ 1]
        both = logsum2([mine, theirs])
        pair_ref[p] = both
        if p % 2 == 0:
            k = p // 2
            mean = even_ref[k] * jnp.exp2(mine - both) + other_ref[k] * jnp.exp2(theirs - both)
            if k == 0:
                own_ref[...] = mean
            else:
                send_refs[k - 1][...] = mean.astype(BF16)


def docs_kernel(groups, place, e_ref, qt_ref, top_ref, weight_ref, pair_ref, *refs):
    far = refs[: groups - 1]
    share_ref, own_ref = refs[groups - 1 : groups + 1]
    send_refs, fq_ref = refs[groups + 1 : -1], refs[-1]
    nb, nd, blk = e_ref.shape
    width = qt_ref.shape[1]
    me, row = place[0], place[1]
    for p in range(nb):
        parts = [pair_ref[p]] + [far[k - 1][p ^ (2 * k)] for k in range(1, groups)]
        whole = logsum2(parts)
        weight = weight_ref[me ^ p]
        if p == 0:
            for k in range(groups):
                lse_k = pair_ref[0] if k == 0 else far[k - 1][2 * k]
                share_ref[k] = weight * jnp.exp2(lse_k - whole)
        scaled = qt_ref[p].astype(F32) * (weight * jnp.exp2(top_ref[p] - whole))
        high = scaled.astype(BF16)
        fq_ref[p, :width, :] = high
        fq_ref[p, width:, :] = (scaled - high.astype(F32)).astype(BF16)
    sub = own_ref.shape[0]
    for j in range(nd // sub):
        at = pl.multiple_of((row ^ j) * sub, sub)
        total = sum(nt_dot(e_ref[p, pl.ds(at, sub), :], fq_ref[p]) for p in range(nb))
        total = total[:, :width] + total[:, width:]
        if j == 0:
            own_ref[...] = total
        else:
            send_refs[j - 1][...] = total.astype(BF16)


def query_kernel(share_ref, own_ref, *refs):
    total = share_ref[0] * own_ref[...]
    for k, ref in enumerate(refs[:-1]):
        total += share_ref[k + 1] * ref[...].astype(F32)
    refs[-1][...] = total.T


def call(kernel, name, outs, args, scalars=0, scratch=(), limit=24 << 20):
    whole = pl.BlockSpec(memory_space=pltpu.VMEM)
    scalar = pl.BlockSpec(memory_space=pltpu.SMEM)
    return pl.pallas_call(
        kernel,
        out_shape=tuple(outs),
        in_specs=[scalar] * scalars + [whole] * (len(args) - scalars),
        out_specs=(whole,) * len(outs),
        scratch_shapes=list(scratch),
        compiler_params=pltpu.CompilerParams(vmem_limit_bytes=limit),
        name=name,
    )(*args)


def swap(x, axis, step):
    return lax.ppermute(x, axis, [(i, i ^ step) for i in range(lax.axis_size(axis))])


def shards(queries, documents, cotangent):
    n, width = queries.shape
    nd = documents.shape[0]
    nb, n_row = lax.axis_size("tok"), lax.axis_size("query")
    blk, sub, groups = n // nb, nd // n_row, nb // 2
    place = jnp.stack([lax.axis_index("tok"), lax.axis_index("query")]).astype(jnp.int32)
    weights = jnp.broadcast_to(cotangent[:, None], (cotangent.shape[0], QLEN)).reshape(nb, 1, blk)
    sds = jax.ShapeDtypeStruct
    stat = sds((nb, 1, blk), F32)
    half = sds((groups, width, blk), F32)

    e, qt, even, odd, lse, top = call(
        tile_kernel,
        "tile",
        (pltpu.VMEM((nb, nd, blk), BF16), pltpu.VMEM((nb, width, blk), BF16), half, half, stat, stat),
        (place, queries, documents),
        scalars=1,
        scratch=(pltpu.VMEM((width + 16, nd), BF16), pltpu.VMEM((nd, blk), F32)),
    )
    other_lse, other = swap(lse, "tok", 1), swap(odd, "tok", 1)
    pair, own_q, *send_q = call(
        pair_kernel,
        "pair",
        (stat, sds((width, blk), F32)) + (sds((width, blk), BF16),) * (groups - 1),
        (even, other, lse, other_lse),
    )
    far = [swap(pair, "tok", 2 * k) for k in range(1, groups)]
    got_q = [swap(x, "tok", 2 * (k + 1)) for k, x in enumerate(send_q)]
    share, own_d, *send_d = call(
        functools.partial(docs_kernel, groups),
        "docs",
        (sds((groups, 1, blk), F32), sds((sub, width), F32)) + (sds((sub, width), BF16),) * (n_row - 1),
        (
            place,
            pltpu.with_memory_space_constraint(e, pltpu.VMEM),
            pltpu.with_memory_space_constraint(qt, pltpu.VMEM),
            top,
            weights,
            pair,
            *far,
        ),
        scalars=1,
        scratch=(pltpu.VMEM((nb, 2 * width, blk), BF16),),
    )
    got_d = [swap(x, "query", j + 1) for j, x in enumerate(send_d)]
    (grad_q,) = call(query_kernel, "queries", (sds((blk, width), F32),), (share, own_q, *got_q))
    grad_d = own_d
    for x in got_d:
        grad_d = grad_d + x.astype(F32)
    return grad_q, grad_d[None]


def solution(mesh):
    placed = (P("query", None), P("tok", None), P("query"))
    return jax.shard_map(
        shards,
        mesh=mesh,
        in_specs=placed,
        out_specs=(P(("query", "tok"), None), P("tok", "query", None)),
        check_vma=False,
    )
```

time: 197 us -> 71.2 us (0.36)
  matrix products: 95.5 us -> 0 us
  blocking collectives: 72.6 us -> 0 us
  Pallas kernels: 0 us -> 34 us
  between operations: 15.6 us -> 0.69 us
  starting transfers between devices: 0.08 us -> 14.2 us
  local copies, waits for them, and re-layouts: 3.42 us -> 14.7 us
  other arithmetic: 6.63 us -> 0.83 us
  waiting for transfers between devices: 0.74 us -> 6.52 us
    dot_general x48 -> x0, matrix products: 95.5 us -> none  [the longest x32 53.6 us: doc_terms(): lax.dot_general(scaled, q_rows, (((0,), (0,)), ((), ())), preferred_eleme...]
    pallas_call x0 -> x4, Pallas kernels: none -> 34 us  [call(): pl.pallas_call(kernel, out_shape=tuple(outs), in_specs=[scalar] * scalars...]
    pmax x1 -> x0, blocking collectives: 30.2 us -> none  [shards(): top_all = lax.pmax(row_tops, 'tok')]
    psum x1 -> x0, blocking collectives: 25.9 us -> none  [shards(): total_all = lax.psum(row_totals * jnp.exp(row_tops - top_all), 'tok')]
    all_gather x2 -> x0, blocking collectives: 16.5 us -> none  [the longest x1 8.24 us: shards(): lax.all_gather(log_total, 'query', axis=0, tiled=True)]
    ppermute x0 -> x11, starting transfers between devices: none -> 14.2 us  [swap(): lax.ppermute(x, axis, [(i, i ^ step) for i in range(lax.axis_size(axis))])]
    unnamed x6 -> x8, local copies, waits for them, and re-layouts: 0.68 us -> 13.8 us
    reduce_sum x8 -> x0, other arithmetic: 6.6 us -> none  [local_stats(): row_total = jnp.sum(jnp.exp(scores - row_top[:, None]), axis=1)]
  transfers between devices with their start and end apart: 2 -> 11, of which waited for: 0 -> 5; matrix products, arithmetic and copies ran while one was open for 54% -> 1% of each run, Pallas kernels for 0% -> 8%
where the time goes in v1:
time: 71.2 us; the launch traced here: 71 us
  Pallas kernels  34 us (48%)
  local copies, waits for them, and re-layouts  14.7 us (21%)
  starting transfers between devices  14.2 us (20%)
  waiting for transfers between devices  6.52 us (9%)
  other arithmetic  0.83 us (1%)
    pallas_call x4, Pallas kernels, call(): pl.pallas_call(kernel, out_shape=tuple(outs), in_specs=[scalar] * scalars...  34 us
    ppermute x11, starting transfers between devices, swap(): lax.ppermute(x, axis, [(i, i ^ step) for i in range(lax.axis_size(axis))])  14.2 us
    unnamed x8, local copies, waits for them, and re-layouts  13.8 us
    ppermute x11, waiting for transfers between devices, swap(): lax.ppermute(x, axis, [(i, i ^ step) for i in range(lax.axis_size(axis))])  6.52 us
  transfers between devices with their start and end apart: 11, of which 5 were waited for; matrix products, arithmetic and copies ran while one was open for 1% of the time, Pallas kernels for 8%

profile of v1, /device:TPU:0, one launch (start us, length us, event | category | flops | bytes accessed | tf_op | source)
XLA Modules:
  0.0 71.0 jit_solution(4491572421326988509)
XLA Ops:
  0.6 0.1 pad_add_fusion.place
  0.7 1.2 %copy-done.2 = bf16[4096,128]{1,0:T(8,128)(2,1)S(1)} copy-done((bf16[4096,128]{1,0:T(8,128)(2,1)S(1)}, bf16[4096,128]{1,0:T(8,128)(2,1)}, u32[]{:S(2)}) %copy-start.2) | copy-done | bytes 1048600
  1.9 1.0 %copy-done.3 = bf16[2048,128]{1,0:T(8,128)(2,1)S(1)} copy-done((bf16[2048,128]{1,0:T(8,128)(2,1)S(1)}, bf16[2048,128]{1,0:T(8,128)(2,1)}, u32[]{:S(2)}) %copy-start.3) | copy-done | bytes 524312
  3.0 27.8 %tile.1 = (bf16[8,2048,512]{2,1,0:T(8,128)(2,1)S(1)}, bf16[8,128,512]{2,1,0:T(8,128)(2,1)S(1)}, f32[4,128,512]{2,1,0:T(8,128)S(1)}, f32[4,128,512]{2,1,0:T(8,128...) custom-call(s32[2]{0:T(128)S(1)} %pad_add_fusion.place, bf16[4096,128]{1,0:T(8,128)(2,1)S(1)} %copy-done.2, ...), custom_call_target="tpu_custom_call" | custom-call | tf_op jit(solution)/shard_map/tile/pallas_call | solution.py:148
  30.8 5.7 %copy-done = bf16[8,2048,512]{2,1,0:T(8,128)(2,1)} copy-done((bf16[8,2048,512]{2,1,0:T(8,128)(2,1)}, bf16[8,2048,512]{2,1,0:T(8,128)(2,1)S(1)}, u32[]{:S(2)}) %copy-start) | copy-done | bytes 16777240
  36.6 0.5 collective-permute-start
  37.0 0.1 collective-permute-start.1
  37.1 2.3 %collective-permute-done.1.other_lse_ref = f32[8,1,512]{2,1,0:T(1,128)S(1)} collective-permute-done((f32[8,1,512]{2,1,0:T(1,128)S(1)}, f32[8,1,512]{2,1,0:T(1,128)S(1)}, u32[]{:S(2)}, u32[]{:S(2)}) %collective-permute-start.1) | collective-permute-done | bytes 16416 | tf_op jit(solution)/shard_map/ppermute | solution.py:160
  39.3 0.2 pair.1
  39.5 3.0 %collective-permute-start.5 = (bf16[128,512]{1,0:T(8,128)(2,1)S(1)}, bf16[128,512]{1,0:T(8,128)(2,1)S(1)}, u32[]{:S(2)}, u32[]{:S(2)}) collective-permute-start(bf16[128,512]{1,0:T(8,128)(2,1)S(1)} %get-tuple-element.27), channel_id=1, source_target_pairs={{0,2},{1,3},{2,0},{3,1},{4,6},{5,7},{6,4},{7,5},{8,10},{9,11},{10,... | collective-permute-start | bytes 393224 | tf_op jit(solution)/shard_map/ppermute | solution.py:160
  42.5 0.1 collective-permute-start.2
  42.6 3.0 %collective-permute-start.3 = (f32[8,1,512]{2,1,0:T(1,128)S(1)}, f32[8,1,512]{2,1,0:T(1,128)S(1)}, u32[]{:S(2)}, u32[]{:S(2)}) collective-permute-start(f32[8,1,512]{2,1,0:T(1,128)S(1)} %get-tuple-element.24.pair_ref), channel_id=1, source_target_pairs={{0,4},{1,5},{2,6},{3,7},{4,0},{5,1},{6,2},{7,3},{8,12},{9,13},{10,... | collective-permute-start | bytes 49160 | tf_op jit(solution)/shard_map/ppermute | solution.py:160
  45.6 1.3 %collective-permute-start.4 = (f32[8,1,512]{2,1,0:T(1,128)S(1)}, f32[8,1,512]{2,1,0:T(1,128)S(1)}, u32[]{:S(2)}, u32[]{:S(2)}) collective-permute-start(f32[8,1,512]{2,1,0:T(1,128)S(1)} %get-tuple-element.24.pair_ref), channel_id=1, source_target_pairs={{0,6},{1,7},{2,4},{3,5},{4,2},{5,3},{6,0},{7,1},{8,14},{9,15},{10,... | collective-permute-start | bytes 49160 | tf_op jit(solution)/shard_map/ppermute | solution.py:160
  46.9 0.7 %broadcast_in_dim.13 = f32[8,16]{1,0:T(8,128)S(1)} reshape(f32[128]{0:T(128)} %param.5) | data formatting | bytes 1024 | tf_op jit(solution)/shard_map/broadcast_in_dim | solution.py:169
  47.6 0.1 broadcast_in_dim.14
  47.7 0.1 broadcast_in_dim.15.weight_ref
  47.8 1.8 %collective-permute-start.6 = (bf16[128,512]{1,0:T(8,128)(2,1)S(1)}, bf16[128,512]{1,0:T(8,128)(2,1)S(1)}, u32[]{:S(2)}, u32[]{:S(2)}) collective-permute-start(bf16[128,512]{1,0:T(8,128)(2,1)S(1)} %get-tuple-element.28), channel_id=1, source_target_pairs={{0,4},{1,5},{2,6},{3,7},{4,0},{5,1},{6,2},{7,3},{8,12},{9,13},{10,... | collective-permute-start | bytes 393224 | tf_op jit(solution)/shard_map/ppermute | solution.py:160
  49.6 0.0 collective-permute-done.2.refs_0_
  49.6 1.0 %collective-permute-start.7 = (bf16[128,512]{1,0:T(8,128)(2,1)S(1)}, bf16[128,512]{1,0:T(8,128)(2,1)S(1)}, u32[]{:S(2)}, u32[]{:S(2)}) collective-permute-start(bf16[128,512]{1,0:T(8,128)(2,1)S(1)} %get-tuple-element.29), channel_id=1, source_target_pairs={{0,6},{1,7},{2,4},{3,5},{4,2},{5,3},{6,0},{7,1},{8,14},{9,15},{10,... | collective-permute-start | bytes 393224 | tf_op jit(solution)/shard_map/ppermute | solution.py:160
  50.6 0.0 collective-permute-done.3.refs_1_
  50.6 0.7 collective-permute-done.4.refs_2_
  51.3 5.8 %copy-done.1 = bf16[8,2048,512]{2,1,0:T(8,128)(2,1)S(1)} copy-done((bf16[8,2048,512]{2,1,0:T(8,128)(2,1)S(1)}, bf16[8,2048,512]{2,1,0:T(8,128)(2,1)}, u32[]{:S(2)}) %copy-start.1) | copy-done | bytes 16777240
  57.1 5.1 %docs.1 = (f32[4,1,512]{2,1,0:T(1,128)S(1)}, f32[512,128]{1,0:T(8,128)S(1)}, bf16[512,128]{1,0:T(8,128)(2,1)S(1)}, bf16[512,128]{1,0:T(8,128)(2,1)S(1)}, bf16[512,128]{1,0:T(8,128)(2,1)S(1)}) custom-call(s32[2]{0:T(128)S(1)} %pad_add_fusion.place, bf16[8,2048,512]{2,1,0:T(8,128)(2,1)S(1)} %copy-done.1, bf16[8,128,512]{2,1,0:T(8,128)(2,1)S(1)} %get-tuple-element.19.qt_ref, ...), custom_call_target="tpu_custom_call" | custom-call | tf_op jit(solution)/shard_map/docs/pallas_call | solution.py:148
  62.2 2.5 %collective-permute-start.10 = (bf16[512,128]{1,0:T(8,128)(2,1)S(1)}, bf16[512,128]{1,0:T(8,128)(2,1)S(1)}, u32[]{:S(2)}, u32[]{:S(2)}) collective-permute-start(bf16[512,128]{1,0:T(8,128)(2,1)S(1)} %get-tuple-element.33), channel_id=1, source_target_pairs={{0,24},{8,16},{16,8},{24,0},{1,25},{9,17},{17,9},{25,1},{2,26},{10... | collective-permute-start | bytes 393224 | tf_op jit(solution)/shard_map/ppermute | solution.py:160
  64.7 0.5 collective-permute-start.8
  65.2 0.5 collective-permute-start.9
  65.8 0.0 collective-permute-done.6.refs_1_
  65.8 0.9 %queries.1 = f32[512,128]{1,0:T(8,128)} custom-call(f32[4,1,512]{2,1,0:T(1,128)S(1)} %get-tuple-element.25.share_ref, f32[128,512]{1,0:T(8,128)S(1)} %get-tuple-element.26.own_ref, bf16[128,512]{1,0:T(8,128)(2,1)S(1)} %collective-permute-done.5.refs_0_, bf16[128,512]{1,0:T(8,128)(2,1)S(1)} %collective-permute-done.6.refs_1_, ...), custom_call_target="tpu_custom_call" | custom-call | tf_op jit(solution)/shard_map/queries/pallas_call | solution.py:148
  66.6 1.6 %collective-permute-done.10 = bf16[512,128]{1,0:T(8,128)(2,1)S(1)} collective-permute-done((bf16[512,128]{1,0:T(8,128)(2,1)S(1)}, bf16[512,128]{1,0:T(8,128)(2,1)S(1)}, u32[]{:S(2)}, u32[]{:S(2)}) %collective-permute-start.10) | collective-permute-done | bytes 131104 | tf_op jit(solution)/shard_map/ppermute | solution.py:160
  68.2 1.4 %collective-permute-done.8 = bf16[512,128]{1,0:T(8,128)(2,1)S(1)} collective-permute-done((bf16[512,128]{1,0:T(8,128)(2,1)S(1)}, bf16[512,128]{1,0:T(8,128)(2,1)S(1)}, u32[]{:S(2)}, u32[]{:S(2)}) %collective-permute-start.8) | collective-permute-done | bytes 131104 | tf_op jit(solution)/shard_map/ppermute | solution.py:160
  69.7 0.5 collective-permute-done.9
  70.2 0.8 %add_bitcast_fusion = f32[1,512,128]{2,1,0:T(8,128)} fusion(bf16[512,128]{1,0:T(8,128)(2,1)S(1)} %collective-permute-done.10, bf16[512,128]{1,0:T(8,128)(2,1)S(1)} %collective-permute-done.9, f32[512,128]{1,0:T(8,128)S(1)} %get-tuple-element.30, bf16[512,128]{1,0:T(8,128)(2,1)S(1)} %collective-permute-done.8), kind=kLoop, calls=%fused_computation | loop fusion | flops 393216 | bytes 917504 | tf_op jit(solution)/shard_map/broadcast_in_dim | solution.py:212
  (7 shorter events, 0.0 us)
Async XLA Ops:
  0.7 1.2 %copy-start.2 = (bf16[4096,128]{1,0:T(8,128)(2,1)S(1)}, bf16[4096,128]{1,0:T(8,128)(2,1)}, u32[]{:S(2)}) copy-start(bf16[4096,128]{1,0:T(8,128)(2,1)} %q_ref.1) | copy-start | bytes 3145732
  1.9 1.0 %copy-start.3 = (bf16[2048,128]{1,0:T(8,128)(2,1)S(1)}, bf16[2048,128]{1,0:T(8,128)(2,1)}, u32[]{:S(2)}) copy-start(bf16[2048,128]{1,0:T(8,128)(2,1)} %d_ref.1) | copy-start | bytes 1572868
  30.8 5.7 %copy-start = (bf16[8,2048,512]{2,1,0:T(8,128)(2,1)}, bf16[8,2048,512]{2,1,0:T(8,128)(2,1)S(1)}, u32[]{:S(2)}) copy-start(bf16[8,2048,512]{2,1,0:T(8,128)(2,1)S(1)} %get-tuple-element.18.e_ref) | copy-start | bytes 50331652
  36.6 2.8 %collective-permute-start = (f32[4,128,512]{2,1,0:T(8,128)S(1)}, f32[4,128,512]{2,1,0:T(8,128)S(1)}, u32[]{:S(2)}, u32[]{:S(2)}) collective-permute-start(f32[4,128,512]{2,1,0:T(8,128)S(1)} %get-tuple-element.22), channel_id=1, source_target_pairs={{0,1},{1,0},{2,3},{3,2},{4,5},{5,4},{6,7},{7,6},{8,9},{9,8},{10,11... | collective-permute-start | bytes 3145736 | tf_op jit(solution)/shard_map/ppermute | solution.py:160
  37.0 2.3 %collective-permute-start.1 = (f32[8,1,512]{2,1,0:T(1,128)S(1)}, f32[8,1,512]{2,1,0:T(1,128)S(1)}, u32[]{:S(2)}, u32[]{:S(2)}) collective-permute-start(f32[8,1,512]{2,1,0:T(1,128)S(1)} %get-tuple-element.23.lse_ref), channel_id=1, source_target_pairs={{0,1},{1,0},{2,3},{3,2},{4,5},{5,4},{6,7},{7,6},{8,9},{9,8},{10,11... | collective-permute-start | bytes 49160 | tf_op jit(solution)/shard_map/ppermute | solution.py:160
  39.5 25.7 %collective-permute-start.5 = (bf16[128,512]{1,0:T(8,128)(2,1)S(1)}, bf16[128,512]{1,0:T(8,128)(2,1)S(1)}, u32[]{:S(2)}, u32[]{:S(2)}) collective-permute-start(bf16[128,512]{1,0:T(8,128)(2,1)S(1)} %get-tuple-element.27), channel_id=1, source_target_pairs={{0,2},{1,3},{2,0},{3,1},{4,6},{5,7},{6,4},{7,5},{8,10},{9,11},{10,... | collective-permute-start | bytes 393224 | tf_op jit(solution)/shard_map/ppermute | solution.py:160
  42.5 7.1 %collective-permute-start.2 = (f32[8,1,512]{2,1,0:T(1,128)S(1)}, f32[8,1,512]{2,1,0:T(1,128)S(1)}, u32[]{:S(2)}, u32[]{:S(2)}) collective-permute-start(f32[8,1,512]{2,1,0:T(1,128)S(1)} %get-tuple-element.24.pair_ref), channel_id=1, source_target_pairs={{0,2},{1,3},{2,0},{3,1},{4,6},{5,7},{6,4},{7,5},{8,10},{9,11},{10,... | collective-permute-start | bytes 49160 | tf_op jit(solution)/shard_map/ppermute | solution.py:160
  42.6 8.0 %collective-permute-start.3 = (f32[8,1,512]{2,1,0:T(1,128)S(1)}, f32[8,1,512]{2,1,0:T(1,128)S(1)}, u32[]{:S(2)}, u32[]{:S(2)}) collective-permute-start(f32[8,1,512]{2,1,0:T(1,128)S(1)} %get-tuple-element.24.pair_ref), channel_id=1, source_target_pairs={{0,4},{1,5},{2,6},{3,7},{4,0},{5,1},{6,2},{7,3},{8,12},{9,13},{10,... | collective-permute-start | bytes 49160 | tf_op jit(solution)/shard_map/ppermute | solution.py:160
  45.6 5.7 %collective-permute-start.4 = (f32[8,1,512]{2,1,0:T(1,128)S(1)}, f32[8,1,512]{2,1,0:T(1,128)S(1)}, u32[]{:S(2)}, u32[]{:S(2)}) collective-permute-start(f32[8,1,512]{2,1,0:T(1,128)S(1)} %get-tuple-element.24.pair_ref), channel_id=1, source_target_pairs={{0,6},{1,7},{2,4},{3,5},{4,2},{5,3},{6,0},{7,1},{8,14},{9,15},{10,... | collective-permute-start | bytes 49160 | tf_op jit(solution)/shard_map/ppermute | solution.py:160
  47.8 17.9 %collective-permute-start.6 = (bf16[128,512]{1,0:T(8,128)(2,1)S(1)}, bf16[128,512]{1,0:T(8,128)(2,1)S(1)}, u32[]{:S(2)}, u32[]{:S(2)}) collective-permute-start(bf16[128,512]{1,0:T(8,128)(2,1)S(1)} %get-tuple-element.28), channel_id=1, source_target_pairs={{0,4},{1,5},{2,6},{3,7},{4,0},{5,1},{6,2},{7,3},{8,12},{9,13},{10,... | collective-permute-start | bytes 393224 | tf_op jit(solution)/shard_map/ppermute | solution.py:160
  49.6 16.2 %collective-permute-start.7 = (bf16[128,512]{1,0:T(8,128)(2,1)S(1)}, bf16[128,512]{1,0:T(8,128)(2,1)S(1)}, u32[]{:S(2)}, u32[]{:S(2)}) collective-permute-start(bf16[128,512]{1,0:T(8,128)(2,1)S(1)} %get-tuple-element.29), channel_id=1, source_target_pairs={{0,6},{1,7},{2,4},{3,5},{4,2},{5,3},{6,0},{7,1},{8,14},{9,15},{10,... | collective-permute-start | bytes 393224 | tf_op jit(solution)/shard_map/ppermute | solution.py:160
  51.3 5.8 %copy-start.1 = (bf16[8,2048,512]{2,1,0:T(8,128)(2,1)S(1)}, bf16[8,2048,512]{2,1,0:T(8,128)(2,1)}, u32[]{:S(2)}) copy-start(bf16[8,2048,512]{2,1,0:T(8,128)(2,1)} %copy-done) | copy-start | bytes 50331652
  62.2 6.0 %collective-permute-start.10 = (bf16[512,128]{1,0:T(8,128)(2,1)S(1)}, bf16[512,128]{1,0:T(8,128)(2,1)S(1)}, u32[]{:S(2)}, u32[]{:S(2)}) collective-permute-start(bf16[512,128]{1,0:T(8,128)(2,1)S(1)} %get-tuple-element.33), channel_id=1, source_target_pairs={{0,24},{8,16},{16,8},{24,0},{1,25},{9,17},{17,9},{25,1},{2,26},{10... | collective-permute-start | bytes 393224 | tf_op jit(solution)/shard_map/ppermute | solution.py:160
  64.7 5.0 %collective-permute-start.8 = (bf16[512,128]{1,0:T(8,128)(2,1)S(1)}, bf16[512,128]{1,0:T(8,128)(2,1)S(1)}, u32[]{:S(2)}, u32[]{:S(2)}) collective-permute-start(bf16[512,128]{1,0:T(8,128)(2,1)S(1)} %get-tuple-element.31), channel_id=1, source_target_pairs={{0,8},{8,0},{16,24},{24,16},{1,9},{9,1},{17,25},{25,17},{2,10},{10... | collective-permute-start | bytes 393224 | tf_op jit(solution)/shard_map/ppermute | solution.py:160
  65.2 5.0 %collective-permute-start.9 = (bf16[512,128]{1,0:T(8,128)(2,1)S(1)}, bf16[512,128]{1,0:T(8,128)(2,1)S(1)}, u32[]{:S(2)}, u32[]{:S(2)}) collective-permute-start(bf16[512,128]{1,0:T(8,128)(2,1)S(1)} %get-tuple-element.32), channel_id=1, source_target_pairs={{0,16},{8,24},{16,0},{24,8},{1,17},{9,25},{17,1},{25,9},{2,18},{10... | collective-permute-start | bytes 393224 | tf_op jit(solution)/shard_map/ppermute | solution.py:160

commit v2 on v1

v2 whole, which is shorter than its diff:
```python
import functools

import jax
import jax.numpy as jnp
from jax import lax
from jax.experimental import pallas as pl
from jax.experimental.pallas import tpu as pltpu
from jax.sharding import PartitionSpec as P

QLEN = 32
SCALE = 2.0 * 1.4426950408889634
ROOM = 30.0
COLUMNS = 1024
DOCS = 512
SAMPLE = 128
F32 = jnp.float32
BF16 = jnp.bfloat16
VMEM = pltpu.VMEM


def nt_dot(a, b):
    return lax.dot_general(a, b, (((1,), (1,)), ((), ())), preferred_element_type=F32)


def nn_dot(a, b):
    return lax.dot_general(a, b, (((1,), (0,)), ((), ())), preferred_element_type=F32)


def logsum2(terms):
    top = functools.reduce(jnp.maximum, terms)
    return top + jnp.log2(sum(jnp.exp2(t - top) for t in terms))


def column_max(s):
    rows, cols = s.shape
    return jnp.max(jnp.max(s.reshape(rows // 8, 8, cols), axis=0), axis=0, keepdims=True)


def tile_kernel(
    cot_ref, q_hbm, d_hbm, e_ref, qt_ref, weight_ref, even_ref, odd_ref, lse_ref, top_ref, q_ref, d_ref, dt_ref, s_ref, sems
):
    groups, nd, cols = e_ref.shape
    n, width = q_ref.shape
    nb = lax.axis_size("tok")
    me = lax.axis_index("tok")
    blk, half = n // nb, nb // 2
    step = min(DOCS, nd)
    sample = min(SAMPLE, nd)

    def block_of(slot):
        return me ^ jnp.where(slot < half, 2 * slot + 1, 2 * (slot - half))

    copies = [pltpu.make_async_copy(d_hbm, d_ref, sems.at[nb])]
    for slot in range(nb):
        source = q_hbm.at[pl.ds(pl.multiple_of(block_of(slot) * blk, blk), blk), :]
        copies.append(pltpu.make_async_copy(source, q_ref.at[slot * blk : (slot + 1) * blk, :], sems.at[slot]))
    for copy in copies:
        copy.start()

    query = lax.broadcasted_iota(jnp.int32, (1, blk), 1) // QLEN
    for slot in range(nb):
        first = block_of(slot) * (blk // QLEN)
        row = jnp.zeros((1, blk), F32)
        for at in range(blk // QLEN):
            row = jnp.where(query == at, cot_ref[first + at], row)
        group, lane = divmod(slot * blk, cols)
        weight_ref[group, :, lane : lane + blk] = row

    copies[0].wait()
    dt_ref[:width, :] = d_ref[...].T
    extra = (dt_ref.shape[0] - width, nd)
    dt_ref[width:, :] = jnp.where(lax.broadcasted_iota(jnp.int32, extra, 0) == 0, 1.0, 0.0).astype(BF16)
    for copy in copies[1:]:
        copy.wait()

    for g in range(groups):
        rows = q_ref[g * cols : (g + 1) * cols, :]
        qt_ref[g] = rows.T
        top_ref[g] = column_max(nt_dot(d_ref[:sample, :], rows)) * SCALE

    def finish(g):
        total = nn_dot(dt_ref[...], e_ref[g])
        mass = total[width : width + 1, :]
        mean = total[:width, :] * (1.0 / mass)

        @pl.when(g < groups // 2)
        def _():
            odd_ref[g] = mean.astype(BF16)

        @pl.when(g >= groups // 2)
        def _():
            even_ref[g - groups // 2] = mean

        spread = jnp.log2(mass)
        lse_ref[g] = top_ref[g] + spread
        return spread

    def quick(g, carry):
        rows = q_ref[pl.ds(pl.multiple_of(g * cols, cols), cols), :]
        top = top_ref[g]
        for at in range(0, nd, step):
            s = nt_dot(d_ref[at : at + step, :], rows)
            e_ref[g, at : at + step, :] = jnp.exp2(s * SCALE - top).astype(BF16)
        return jnp.maximum(carry, finish(g))

    spread = lax.fori_loop(0, groups, quick, jnp.zeros((1, cols), F32))

    @pl.when(jnp.logical_not(jnp.max(spread) <= ROOM))
    def _():
        def careful(g, carry):
            rows = q_ref[pl.ds(pl.multiple_of(g * cols, cols), cols), :]
            top = None
            for at in range(0, nd, step):
                s = nt_dot(d_ref[at : at + step, :], rows)
                s_ref[at : at + step, :] = s
                here = column_max(s)
                top = here if top is None else jnp.maximum(top, here)
            top = top * SCALE
            top_ref[g] = top
            for at in range(0, nd, step):
                e_ref[g, at : at + step, :] = jnp.exp2(s_ref[at : at + step, :] * SCALE - top).astype(BF16)
            finish(g)
            return carry

        lax.fori_loop(0, groups, careful, 0)


def pair_kernel(even_ref, other_ref, lse_ref, other_lse_ref, pair_ref, own_ref, *send_refs):
    groups = lse_ref.shape[0]
    width, blk = own_ref.shape
    for g in range(groups):
        mine, theirs = lse_ref[g], other_lse_ref[(g + groups // 2) % groups]
        both = logsum2([mine, theirs])
        pair_ref[g] = both
        if g >= groups // 2:
            h = g - groups // 2
            mean = even_ref[h] * jnp.exp2(mine - both) + other_ref[h].astype(F32) * jnp.exp2(theirs - both)
            per = mean.shape[1] // blk
            for i in range(per):
                k, part = h * per + i, mean[:, i * blk : (i + 1) * blk]
                if k == 0:
                    own_ref[...] = part
                else:
                    send_refs[k - 1][...] = part.astype(BF16)


def docs_kernel(chips, e_ref, qt_ref, top_ref, weight_ref, pair_ref, *refs):
    far = refs[: chips - 1]
    share_ref, own_ref = refs[chips - 1 : chips + 1]
    send_refs, fq_ref = refs[chips + 1 : -1], refs[-1]
    groups, nd, cols = e_ref.shape
    width = qt_ref.shape[1]
    blk = share_ref.shape[2]
    row = lax.axis_index("query")

    def slot_of(ref, slot):
        group, lane = divmod(slot * blk, cols)
        return ref[group, :, lane : lane + blk]

    for slot in range(groups * cols // blk):
        base, k = divmod(slot, chips)
        base *= chips
        parts = [slot_of(pair_ref, slot)] + [slot_of(far[z - 1], base + (k ^ z)) for z in range(1, chips)]
        whole = logsum2(parts)
        weight = slot_of(weight_ref, slot)
        if slot == chips:
            for z in range(chips):
                share_ref[z] = weight * jnp.exp2(parts[z] - whole)
        group, lane = divmod(slot * blk, cols)
        factor = weight * jnp.exp2(slot_of(top_ref, slot) - whole)
        scaled = qt_ref[group, :, lane : lane + blk].astype(F32) * factor
        high = scaled.astype(BF16)
        fq_ref[group, :width, lane : lane + blk] = high
        fq_ref[group, width:, lane : lane + blk] = (scaled - high.astype(F32)).astype(BF16)
    sub = own_ref.shape[0]
    for j in range(nd // sub):
        at = pl.multiple_of((row ^ j) * sub, sub)
        total = sum(nt_dot(e_ref[g, pl.ds(at, sub), :], fq_ref[g]) for g in range(groups))
        total = total[:, :width] + total[:, width:]
        if j == 0:
            own_ref[...] = total
        else:
            send_refs[j - 1][...] = total.astype(BF16)


def query_kernel(share_ref, own_ref, *refs):
    total = share_ref[0] * own_ref[...]
    for k, ref in enumerate(refs[:-1]):
        total += share_ref[k + 1] * ref[...].astype(F32)
    refs[-1][...] = total.T


def call(kernel, name, outs, args, spaces=None, scratch=(), limit=12 << 20):
    spaces = spaces or [VMEM] * len(args)
    return pl.pallas_call(
        kernel,
        out_shape=tuple(outs),
        in_specs=[pl.BlockSpec(memory_space=space) for space in spaces],
        out_specs=(pl.BlockSpec(memory_space=VMEM),) * len(outs),
        scratch_shapes=list(scratch),
        compiler_params=pltpu.CompilerParams(vmem_limit_bytes=limit),
        name=name,
    )(*args)


def swap(x, axis, step):
    return lax.ppermute(x, axis, [(i, i ^ step) for i in range(lax.axis_size(axis))])


def shards(queries, documents, cotangent):
    n, width = queries.shape
    nd = documents.shape[0]
    nb, n_row = lax.axis_size("tok"), lax.axis_size("query")
    chips = nb // 2
    blk, sub = n // nb, nd // n_row
    cols = min(max(COLUMNS, blk), n // 2)
    groups = n // cols
    sds = jax.ShapeDtypeStruct
    stat = sds((groups, 1, cols), F32)

    e, qt, weight, even, odd, lse, top = call(
        tile_kernel,
        "tile",
        (
            VMEM((groups, nd, cols), BF16),
            VMEM((groups, width, cols), BF16),
            stat,
            sds((groups // 2, width, cols), F32),
            sds((groups // 2, width, cols), BF16),
            stat,
            stat,
        ),
        (cotangent, pltpu.with_memory_space_constraint(queries, pltpu.HBM), pltpu.with_memory_space_constraint(documents, pltpu.HBM)),
        spaces=(pltpu.SMEM, pltpu.HBM, pltpu.HBM),
        scratch=(
            VMEM((n, width), BF16),
            VMEM((nd, width), BF16),
            VMEM((width + 16, nd), BF16),
            VMEM((nd, cols), F32),
            pltpu.SemaphoreType.DMA((nb + 1,)),
        ),
        limit=16 << 20,
    )
    other_lse, other = swap(lse, "tok", 1), swap(odd, "tok", 1)
    pair, own_q, *send_q = call(
        pair_kernel,
        "pair",
        (stat, sds((width, blk), F32)) + (sds((width, blk), BF16),) * (chips - 1),
        (even, other, lse, other_lse),
    )
    far = [swap(pair, "tok", 2 * k) for k in range(1, chips)]
    got_q = [swap(x, "tok", 2 * (k + 1)) for k, x in enumerate(send_q)]
    share, own_d, *send_d = call(
        functools.partial(docs_kernel, chips),
        "docs",
        (sds((chips, 1, blk), F32), sds((sub, width), F32)) + (sds((sub, width), BF16),) * (n_row - 1),
        (
            pltpu.with_memory_space_constraint(e, VMEM),
            pltpu.with_memory_space_constraint(qt, VMEM),
            top,
            weight,
            pair,
            *far,
        ),
        scratch=(VMEM((groups, 2 * width, cols), BF16),),
    )
    got_d = [swap(x, "query", j + 1) for j, x in enumerate(send_d)]
    (grad_q,) = call(query_kernel, "queries", (sds((blk, width), F32),), (share, own_q, *got_q))
    grad_d = own_d
    for x in got_d:
        grad_d = grad_d + x.astype(F32)
    return grad_q, grad_d[None]


def solution(mesh):
    placed = (P("query", None), P("tok", None), P("query"))
    return jax.shard_map(
        shards,
        mesh=mesh,
        in_specs=placed,
        out_specs=(P(("query", "tok"), None), P("tok", "query", None)),
        check_vma=False,
    )
```

time: 71.2 us -> 58 us (0.81)
  local copies, waits for them, and re-layouts: 14.7 us -> 0.65 us
  waiting for transfers between devices: 6.52 us -> 10 us
  Pallas kernels: 34 us -> 30.9 us
    unnamed x8 -> x2, local copies, waits for them, and re-layouts: 13.8 us -> 0.65 us
    ppermute x11, waiting for transfers between devices: 6.52 us -> 10 us  [swap(): lax.ppermute(x, axis, [(i, i ^ step) for i in range(lax.axis_size(axis))])]
    pallas_call x4, Pallas kernels: 34 us -> 30.9 us  [call(): pl.pallas_call(kernel, out_shape=tuple(outs), in_specs=[pl.BlockSpec(memo...]
    broadcast_in_dim x3 -> x0, local copies, waits for them, and re-layouts: 0.91 us -> none  [shards(): jnp.broadcast_to(cotangent[:, None], (cotangent.shape[0], QLEN))]
  transfers between devices with their start and end apart: 11 -> 11, of which waited for: 5 -> 6; matrix products, arithmetic and copies ran while one was open for 1% -> 0% of each run, Pallas kernels for 8% -> 9%
where the time goes in v2:
time: 58 us; the launch traced here: 57.8 us
  Pallas kernels  30.9 us (53%)
  starting transfers between devices  14.8 us (26%)
  waiting for transfers between devices  10 us (17%)
  other arithmetic  0.76 us (1%)
  between operations  0.67 us (1%)
  local copies, waits for them, and re-layouts  0.65 us (1%)
    pallas_call x4, Pallas kernels, call(): pl.pallas_call(kernel, out_shape=tuple(outs), in_specs=[pl.BlockSpec(memo...  30.9 us
    ppermute x11, starting transfers between devices, swap(): lax.ppermute(x, axis, [(i, i ^ step) for i in range(lax.axis_size(axis))])  14.8 us
    ppermute x11, waiting for transfers between devices, swap(): lax.ppermute(x, axis, [(i, i ^ step) for i in range(lax.axis_size(axis))])  10 us
  transfers between devices with their start and end apart: 11, of which 6 were waited for; matrix products, arithmetic and copies ran while one was open for 0% of the time, Pallas kernels for 9%

profile of v2, /device:TPU:0, one launch (start us, length us, event | category | flops | bytes accessed | tf_op | source)
XLA Modules:
  0.0 57.8 jit_solution(15300794528860304858)
XLA Ops:
  0.6 0.0 copy-start
  0.6 0.6 %copy-done = f32[128]{0:T(128)S(1)} copy-done((f32[128]{0:T(128)S(1)}, f32[128]{0:T(128)}, u32[]{:S(2)}) %copy-start) | copy-done | bytes 536
  1.3 25.3 %tile.1 = (bf16[4,2048,1024]{2,1,0:T(8,128)(2,1)S(1)}, bf16[4,128,1024]{2,1,0:T(8,128)(2,1)S(1)}, f32[4,1,1024]{2,1,0:T(1,128)S(1)}, f32[2,128,1024]{2,1,0:T(8,1...) custom-call(f32[128]{0:T(128)S(1)} %copy-done, ...), custom_call_target="tpu_custom_call" | custom-call | tf_op jit(solution)/shard_map/tile/pallas_call | solution.py:195
  26.6 0.5 collective-permute-start
  27.1 0.1 collective-permute-start.1
  27.2 1.5 %collective-permute-done.1.other_lse_ref = f32[4,1,1024]{2,1,0:T(1,128)S(1)} collective-permute-done((f32[4,1,1024]{2,1,0:T(1,128)S(1)}, f32[4,1,1024]{2,1,0:T(1,128)S(1)}, u32[]{:S(2)}, u32[]{:S(2)}) %collective-permute-start.1) | collective-permute-done | bytes 16416 | tf_op jit(solution)/shard_map/ppermute | solution.py:207
  28.7 0.0 collective-permute-done.other_ref
  28.7 0.2 pair.1
  28.9 3.0 %collective-permute-start.5 = (bf16[128,512]{1,0:T(8,128)(2,1)S(1)}, bf16[128,512]{1,0:T(8,128)(2,1)S(1)}, u32[]{:S(2)}, u32[]{:S(2)}) collective-permute-start(bf16[128,512]{1,0:T(8,128)(2,1)S(1)} %get-tuple-element.29), channel_id=1, source_target_pairs={{0,2},{1,3},{2,0},{3,1},{4,6},{5,7},{6,4},{7,5},{8,10},{9,11},{10,... | collective-permute-start | bytes 393224 | tf_op jit(solution)/shard_map/ppermute | solution.py:207
  31.9 2.5 %collective-permute-start.4 = (f32[4,1,1024]{2,1,0:T(1,128)S(1)}, f32[4,1,1024]{2,1,0:T(1,128)S(1)}, u32[]{:S(2)}, u32[]{:S(2)}) collective-permute-start(f32[4,1,1024]{2,1,0:T(1,128)S(1)} %get-tuple-element.26.pair_ref), channel_id=1, source_target_pairs={{0,6},{1,7},{2,4},{3,5},{4,2},{5,3},{6,0},{7,1},{8,14},{9,15},{10,... | collective-permute-start | bytes 49160 | tf_op jit(solution)/shard_map/ppermute | solution.py:207
  34.4 0.1 collective-permute-start.3
  34.5 1.8 %collective-permute-start.2 = (f32[4,1,1024]{2,1,0:T(1,128)S(1)}, f32[4,1,1024]{2,1,0:T(1,128)S(1)}, u32[]{:S(2)}, u32[]{:S(2)}) collective-permute-start(f32[4,1,1024]{2,1,0:T(1,128)S(1)} %get-tuple-element.26.pair_ref), channel_id=1, source_target_pairs={{0,2},{1,3},{2,0},{3,1},{4,6},{5,7},{6,4},{7,5},{8,10},{9,11},{10,... | collective-permute-start | bytes 49160 | tf_op jit(solution)/shard_map/ppermute | solution.py:207
  36.3 1.7 %collective-permute-start.6 = (bf16[128,512]{1,0:T(8,128)(2,1)S(1)}, bf16[128,512]{1,0:T(8,128)(2,1)S(1)}, u32[]{:S(2)}, u32[]{:S(2)}) collective-permute-start(bf16[128,512]{1,0:T(8,128)(2,1)S(1)} %get-tuple-element.30), channel_id=1, source_target_pairs={{0,4},{1,5},{2,6},{3,7},{4,0},{5,1},{6,2},{7,3},{8,12},{9,13},{10,... | collective-permute-start | bytes 393224 | tf_op jit(solution)/shard_map/ppermute | solution.py:207
  38.0 0.4 collective-permute-done.4.refs_2_
  38.4 1.5 %collective-permute-start.7 = (bf16[128,512]{1,0:T(8,128)(2,1)S(1)}, bf16[128,512]{1,0:T(8,128)(2,1)S(1)}, u32[]{:S(2)}, u32[]{:S(2)}) collective-permute-start(bf16[128,512]{1,0:T(8,128)(2,1)S(1)} %get-tuple-element.31), channel_id=1, source_target_pairs={{0,6},{1,7},{2,4},{3,5},{4,2},{5,3},{6,0},{7,1},{8,14},{9,15},{10,... | collective-permute-start | bytes 393224 | tf_op jit(solution)/shard_map/ppermute | solution.py:207
  39.9 3.6 %collective-permute-done.3.refs_1_ = f32[4,1,1024]{2,1,0:T(1,128)S(1)} collective-permute-done((f32[4,1,1024]{2,1,0:T(1,128)S(1)}, f32[4,1,1024]{2,1,0:T(1,128)S(1)}, u32[]{:S(2)}, u32[]{:S(2)}) %collective-permute-start.3) | collective-permute-done | bytes 16416 | tf_op jit(solution)/shard_map/ppermute | solution.py:207
  43.6 0.0 collective-permute-done.2.refs_0_
  43.6 4.6 %docs.1 = (f32[4,1,512]{2,1,0:T(1,128)S(1)}, f32[512,128]{1,0:T(8,128)S(1)}, bf16[512,128]{1,0:T(8,128)(2,1)S(1)}, bf16[512,128]{1,0:T(8,128)(2,1)S(1)}, bf16[512,128]{1,0:T(8,128)(2,1)S(1)}) custom-call(bf16[4,2048,1024]{2,1,0:T(8,128)(2,1)S(1)} %get-tuple-element.19.e_ref, bf16[4,128,1024]{2,1,0:T(8,128)(2,1)S(1)} %get-tuple-element.20.qt_ref, ...), custom_call_target="tpu_custom_call" | custom-call | tf_op jit(solution)/shard_map/docs/pallas_call | solution.py:195
  48.1 1.6 %collective-permute-start.8 = (bf16[512,128]{1,0:T(8,128)(2,1)S(1)}, bf16[512,128]{1,0:T(8,128)(2,1)S(1)}, u32[]{:S(2)}, u32[]{:S(2)}) collective-permute-start(bf16[512,128]{1,0:T(8,128)(2,1)S(1)} %get-tuple-element.33), channel_id=1, source_target_pairs={{0,8},{8,0},{16,24},{24,16},{1,9},{9,1},{17,25},{25,17},{2,10},{10... | collective-permute-start | bytes 393224 | tf_op jit(solution)/shard_map/ppermute | solution.py:207
  49.7 1.5 %collective-permute-start.9 = (bf16[512,128]{1,0:T(8,128)(2,1)S(1)}, bf16[512,128]{1,0:T(8,128)(2,1)S(1)}, u32[]{:S(2)}, u32[]{:S(2)}) collective-permute-start(bf16[512,128]{1,0:T(8,128)(2,1)S(1)} %get-tuple-element.34), channel_id=1, source_target_pairs={{0,16},{8,24},{16,0},{24,8},{1,17},{9,25},{17,1},{25,9},{2,18},{10... | collective-permute-start | bytes 393224 | tf_op jit(solution)/shard_map/ppermute | solution.py:207
  51.2 0.0 collective-permute-done.5.refs_0_
  51.2 0.5 collective-permute-start.10
  51.7 0.0 collective-permute-done.6.refs_1_
  51.7 0.0 collective-permute-done.7.refs_2_
  51.7 0.9 %queries.1 = f32[512,128]{1,0:T(8,128)} custom-call(f32[4,1,512]{2,1,0:T(1,128)S(1)} %get-tuple-element.27.share_ref, f32[128,512]{1,0:T(8,128)S(1)} %get-tuple-element.28.own_ref, bf16[128,512]{1,0:T(8,128)(2,1)S(1)} %collective-permute-done.5.refs_0_, bf16[128,512]{1,0:T(8,128)(2,1)S(1)} %collective-permute-done.6.refs_1_, ...), custom_call_target="tpu_custom_call" | custom-call | tf_op jit(solution)/shard_map/queries/pallas_call | solution.py:195
  52.6 0.6 %collective-permute-done.8 = bf16[512,128]{1,0:T(8,128)(2,1)S(1)} collective-permute-done((bf16[512,128]{1,0:T(8,128)(2,1)S(1)}, bf16[512,128]{1,0:T(8,128)(2,1)S(1)}, u32[]{:S(2)}, u32[]{:S(2)}) %collective-permute-start.8) | collective-permute-done | bytes 131104 | tf_op jit(solution)/shard_map/ppermute | solution.py:207
  53.2 1.5 %collective-permute-done.9 = bf16[512,128]{1,0:T(8,128)(2,1)S(1)} collective-permute-done((bf16[512,128]{1,0:T(8,128)(2,1)S(1)}, bf16[512,128]{1,0:T(8,128)(2,1)S(1)}, u32[]{:S(2)}, u32[]{:S(2)}) %collective-permute-start.9) | collective-permute-done | bytes 131104 | tf_op jit(solution)/shard_map/ppermute | solution.py:207
  54.7 2.4 %collective-permute-done.10 = bf16[512,128]{1,0:T(8,128)(2,1)S(1)} collective-permute-done((bf16[512,128]{1,0:T(8,128)(2,1)S(1)}, bf16[512,128]{1,0:T(8,128)(2,1)S(1)}, u32[]{:S(2)}, u32[]{:S(2)}) %collective-permute-start.10) | collective-permute-done | bytes 131104 | tf_op jit(solution)/shard_map/ppermute | solution.py:207
  57.1 0.8 %add_bitcast_fusion = f32[1,512,128]{2,1,0:T(8,128)} fusion(bf16[512,128]{1,0:T(8,128)(2,1)S(1)} %collective-permute-done.10, bf16[512,128]{1,0:T(8,128)(2,1)S(1)} %collective-permute-done.9, f32[512,128]{1,0:T(8,128)S(1)} %get-tuple-element.32, bf16[512,128]{1,0:T(8,128)(2,1)S(1)} %collective-permute-done.8), kind=kLoop, calls=%fused_computation | loop fusion | flops 393216 | bytes 917504 | tf_op jit(solution)/shard_map/broadcast_in_dim | solution.py:272
Async XLA Ops:
  0.6 0.7 %copy-start = (f32[128]{0:T(128)S(1)}, f32[128]{0:T(128)}, u32[]{:S(2)}) copy-start(f32[128]{0:T(128)} %cot_ref.1) | copy-start | bytes 1540
  26.6 2.1 %collective-permute-start = (bf16[2,128,1024]{2,1,0:T(8,128)(2,1)S(1)}, bf16[2,128,1024]{2,1,0:T(8,128)(2,1)S(1)}, u32[]{:S(2)}, u32[]{:S(2)}) collective-permute-start(bf16[2,128,1024]{2,1,0:T(8,128)(2,1)S(1)} %get-tuple-element.24), channel_id=1, source_target_pairs={{0,1},{1,0},{2,3},{3,2},{4,5},{5,4},{6,7},{7,6},{8,9},{9,8},{10,11... | collective-permute-start | bytes 1572872 | tf_op jit(solution)/shard_map/ppermute | solution.py:207
  27.1 1.6 %collective-permute-start.1 = (f32[4,1,1024]{2,1,0:T(1,128)S(1)}, f32[4,1,1024]{2,1,0:T(1,128)S(1)}, u32[]{:S(2)}, u32[]{:S(2)}) collective-permute-start(f32[4,1,1024]{2,1,0:T(1,128)S(1)} %get-tuple-element.25.lse_ref), channel_id=1, source_target_pairs={{0,1},{1,0},{2,3},{3,2},{4,5},{5,4},{6,7},{7,6},{8,9},{9,8},{10,11... | collective-permute-start | bytes 49160 | tf_op jit(solution)/shard_map/ppermute | solution.py:207
  28.9 22.3 %collective-permute-start.5 = (bf16[128,512]{1,0:T(8,128)(2,1)S(1)}, bf16[128,512]{1,0:T(8,128)(2,1)S(1)}, u32[]{:S(2)}, u32[]{:S(2)}) collective-permute-start(bf16[128,512]{1,0:T(8,128)(2,1)S(1)} %get-tuple-element.29), channel_id=1, source_target_pairs={{0,2},{1,3},{2,0},{3,1},{4,6},{5,7},{6,4},{7,5},{8,10},{9,11},{10,... | collective-permute-start | bytes 393224 | tf_op jit(solution)/shard_map/ppermute | solution.py:207
  31.9 6.5 %collective-permute-start.4 = (f32[4,1,1024]{2,1,0:T(1,128)S(1)}, f32[4,1,1024]{2,1,0:T(1,128)S(1)}, u32[]{:S(2)}, u32[]{:S(2)}) collective-permute-start(f32[4,1,1024]{2,1,0:T(1,128)S(1)} %get-tuple-element.26.pair_ref), channel_id=1, source_target_pairs={{0,6},{1,7},{2,4},{3,5},{4,2},{5,3},{6,0},{7,1},{8,14},{9,15},{10,... | collective-permute-start | bytes 49160 | tf_op jit(solution)/shard_map/ppermute | solution.py:207
  34.4 9.2 %collective-permute-start.3 = (f32[4,1,1024]{2,1,0:T(1,128)S(1)}, f32[4,1,1024]{2,1,0:T(1,128)S(1)}, u32[]{:S(2)}, u32[]{:S(2)}) collective-permute-start(f32[4,1,1024]{2,1,0:T(1,128)S(1)} %get-tuple-element.26.pair_ref), channel_id=1, source_target_pairs={{0,4},{1,5},{2,6},{3,7},{4,0},{5,1},{6,2},{7,3},{8,12},{9,13},{10,... | collective-permute-start | bytes 49160 | tf_op jit(solution)/shard_map/ppermute | solution.py:207
  34.5 9.1 %collective-permute-start.2 = (f32[4,1,1024]{2,1,0:T(1,128)S(1)}, f32[4,1,1024]{2,1,0:T(1,128)S(1)}, u32[]{:S(2)}, u32[]{:S(2)}) collective-permute-start(f32[4,1,1024]{2,1,0:T(1,128)S(1)} %get-tuple-element.26.pair_ref), channel_id=1, source_target_pairs={{0,2},{1,3},{2,0},{3,1},{4,6},{5,7},{6,4},{7,5},{8,10},{9,11},{10,... | collective-permute-start | bytes 49160 | tf_op jit(solution)/shard_map/ppermute | solution.py:207
  36.3 15.4 %collective-permute-start.6 = (bf16[128,512]{1,0:T(8,128)(2,1)S(1)}, bf16[128,512]{1,0:T(8,128)(2,1)S(1)}, u32[]{:S(2)}, u32[]{:S(2)}) collective-permute-start(bf16[128,512]{1,0:T(8,128)(2,1)S(1)} %get-tuple-element.30), channel_id=1, source_target_pairs={{0,4},{1,5},{2,6},{3,7},{4,0},{5,1},{6,2},{7,3},{8,12},{9,13},{10,... | collective-permute-start | bytes 393224 | tf_op jit(solution)/shard_map/ppermute | solution.py:207
  38.4 13.3 %collective-permute-start.7 = (bf16[128,512]{1,0:T(8,128)(2,1)S(1)}, bf16[128,512]{1,0:T(8,128)(2,1)S(1)}, u32[]{:S(2)}, u32[]{:S(2)}) collective-permute-start(bf16[128,512]{1,0:T(8,128)(2,1)S(1)} %get-tuple-element.31), channel_id=1, source_target_pairs={{0,6},{1,7},{2,4},{3,5},{4,2},{5,3},{6,0},{7,1},{8,14},{9,15},{10,... | collective-permute-start | bytes 393224 | tf_op jit(solution)/shard_map/ppermute | solution.py:207
  48.1 5.0 %collective-permute-start.8 = (bf16[512,128]{1,0:T(8,128)(2,1)S(1)}, bf16[512,128]{1,0:T(8,128)(2,1)S(1)}, u32[]{:S(2)}, u32[]{:S(2)}) collective-permute-start(bf16[512,128]{1,0:T(8,128)(2,1)S(1)} %get-tuple-element.33), channel_id=1, source_target_pairs={{0,8},{8,0},{16,24},{24,16},{1,9},{9,1},{17,25},{25,17},{2,10},{10... | collective-permute-start | bytes 393224 | tf_op jit(solution)/shard_map/ppermute | solution.py:207
  49.7 5.0 %collective-permute-start.9 = (bf16[512,128]{1,0:T(8,128)(2,1)S(1)}, bf16[512,128]{1,0:T(8,128)(2,1)S(1)}, u32[]{:S(2)}, u32[]{:S(2)}) collective-permute-start(bf16[512,128]{1,0:T(8,128)(2,1)S(1)} %get-tuple-element.34), channel_id=1, source_target_pairs={{0,16},{8,24},{16,0},{24,8},{1,17},{9,25},{17,1},{25,9},{2,18},{10... | collective-permute-start | bytes 393224 | tf_op jit(solution)/shard_map/ppermute | solution.py:207
  51.2 5.9 %collective-permute-start.10 = (bf16[512,128]{1,0:T(8,128)(2,1)S(1)}, bf16[512,128]{1,0:T(8,128)(2,1)S(1)}, u32[]{:S(2)}, u32[]{:S(2)}) collective-permute-start(bf16[512,128]{1,0:T(8,128)(2,1)S(1)} %get-tuple-element.35), channel_id=1, source_target_pairs={{0,24},{8,16},{16,8},{24,0},{1,25},{9,17},{17,9},{25,1},{2,26},{10... | collective-permute-start | bytes 393224 | tf_op jit(solution)/shard_map/ppermute | solution.py:207

commit v3 on v2

--- a/solution.py
+++ b/solution.py
@@ -37,7 +37,7 @@
 
 
 def tile_kernel(
-    cot_ref, q_hbm, d_hbm, e_ref, qt_ref, weight_ref, even_ref, odd_ref, lse_ref, top_ref, q_ref, d_ref, dt_ref, s_ref, sems
+    cot_hbm, q_hbm, d_hbm, e_ref, qt_ref, weight_ref, even_ref, odd_ref, lse_ref, top_ref, cot_ref, q_ref, d_ref, dt_ref, s_ref, sems
 ):
     groups, nd, cols = e_ref.shape
     n, width = q_ref.shape
@@ -54,8 +54,11 @@
     for slot in range(nb):
         source = q_hbm.at[pl.ds(pl.multiple_of(block_of(slot) * blk, blk), blk), :]
         copies.append(pltpu.make_async_copy(source, q_ref.at[slot * blk : (slot + 1) * blk, :], sems.at[slot]))
+    copies.append(pltpu.make_async_copy(cot_hbm, cot_ref, sems.at[nb + 1]))
     for copy in copies:
         copy.start()
+    for copy in copies:
+        copy.wait()
 
     query = lax.broadcasted_iota(jnp.int32, (1, blk), 1) // QLEN
     for slot in range(nb):
@@ -66,12 +69,9 @@
         group, lane = divmod(slot * blk, cols)
         weight_ref[group, :, lane : lane + blk] = row
 
-    copies[0].wait()
     dt_ref[:width, :] = d_ref[...].T
     extra = (dt_ref.shape[0] - width, nd)
     dt_ref[width:, :] = jnp.where(lax.broadcasted_iota(jnp.int32, extra, 0) == 0, 1.0, 0.0).astype(BF16)
-    for copy in copies[1:]:
-        copy.wait()
 
     for g in range(groups):
         rows = q_ref[g * cols : (g + 1) * cols, :]
@@ -125,29 +125,33 @@
         lax.fori_loop(0, groups, careful, 0)
 
 
-def pair_kernel(even_ref, other_ref, lse_ref, other_lse_ref, pair_ref, own_ref, *send_refs):
+def pair_kernel(lse_ref, other_lse_ref, pair_ref):
     groups = lse_ref.shape[0]
+    for g in range(groups):
+        pair_ref[g] = logsum2([lse_ref[g], other_lse_ref[(g + groups // 2) % groups]])
+
+
+def mean_kernel(even_ref, other_ref, lse_ref, other_lse_ref, pair_ref, own_ref, *send_refs):
     width, blk = own_ref.shape
-    for g in range(groups):
-        mine, theirs = lse_ref[g], other_lse_ref[(g + groups // 2) % groups]
-        both = logsum2([mine, theirs])
-        pair_ref[g] = both
-        if g >= groups // 2:
-            h = g - groups // 2
-            mean = even_ref[h] * jnp.exp2(mine - both) + other_ref[h].astype(F32) * jnp.exp2(theirs - both)
-            per = mean.shape[1] // blk
-            for i in range(per):
-                k, part = h * per + i, mean[:, i * blk : (i + 1) * blk]
-                if k == 0:
-                    own_ref[...] = part
-                else:
-                    send_refs[k - 1][...] = part.astype(BF16)
-
-
-def docs_kernel(chips, e_ref, qt_ref, top_ref, weight_ref, pair_ref, *refs):
+    first = lse_ref.shape[0] // 2
+    for h in range(first):
+        both = pair_ref[first + h]
+        mine, theirs = jnp.exp2(lse_ref[first + h] - both), jnp.exp2(other_lse_ref[h] - both)
+        mean = even_ref[h] * mine + other_ref[h].astype(F32) * theirs
+        per = mean.shape[1] // blk
+        for i in range(per):
+            k, part = h * per + i, mean[:, i * blk : (i + 1) * blk]
+            if k == 0:
+                own_ref[...] = part
+            else:
+                send_refs[k - 1][...] = part.astype(BF16)
+
+
+def docs_kernel(chips, e_ref, qt_ref, top_ref, weight_ref, gate_ref, pair_ref, *refs):
+    del gate_ref
     far = refs[: chips - 1]
-    share_ref, own_ref = refs[chips - 1 : chips + 1]
-    send_refs, fq_ref = refs[chips + 1 : -1], refs[-1]
+    share_ref, fq_ref = refs[chips - 1 : chips + 1]
+    send_refs = refs[chips + 1 :]
     groups, nd, cols = e_ref.shape
     width = qt_ref.shape[1]
     blk = share_ref.shape[2]
@@ -172,15 +176,19 @@
         high = scaled.astype(BF16)
         fq_ref[group, :width, lane : lane + blk] = high
         fq_ref[group, width:, lane : lane + blk] = (scaled - high.astype(F32)).astype(BF16)
-    sub = own_ref.shape[0]
-    for j in range(nd // sub):
-        at = pl.multiple_of((row ^ j) * sub, sub)
-        total = sum(nt_dot(e_ref[g, pl.ds(at, sub), :], fq_ref[g]) for g in range(groups))
-        total = total[:, :width] + total[:, width:]
-        if j == 0:
-            own_ref[...] = total
-        else:
-            send_refs[j - 1][...] = total.astype(BF16)
+    for j, ref in enumerate(send_refs):
+        ref[...] = docs_rows(e_ref, fq_ref, row ^ (j + 1), ref.shape[0]).astype(BF16)
+
+
+def docs_rows(e_ref, fq_ref, at, rows):
+    span = pl.ds(pl.multiple_of(at * rows, rows), rows)
+    total = sum(nt_dot(e_ref[g, span, :], fq_ref[g]) for g in range(e_ref.shape[0]))
+    width = total.shape[1] // 2
+    return total[:, :width] + total[:, width:]
+
+
+def own_docs_kernel(e_ref, fq_ref, own_ref):
+    own_ref[...] = docs_rows(e_ref, fq_ref, lax.axis_index("query"), own_ref.shape[0])
 
 
 def query_kernel(share_ref, own_ref, *refs):
@@ -190,7 +198,7 @@
     refs[-1][...] = total.T
 
 
-def call(kernel, name, outs, args, spaces=None, scratch=(), limit=12 << 20):
+def call(kernel, name, outs, args, spaces=None, scratch=(), limit=12 << 20, cost=None):
     spaces = spaces or [VMEM] * len(args)
     return pl.pallas_call(
         kernel,
@@ -200,6 +208,7 @@
         scratch_shapes=list(scratch),
         compiler_params=pltpu.CompilerParams(vmem_limit_bytes=limit),
         name=name,
+        cost_estimate=cost,
     )(*args)
 
 
@@ -230,41 +239,44 @@
             stat,
             stat,
         ),
-        (cotangent, pltpu.with_memory_space_constraint(queries, pltpu.HBM), pltpu.with_memory_space_constraint(documents, pltpu.HBM)),
-        spaces=(pltpu.SMEM, pltpu.HBM, pltpu.HBM),
+        [pltpu.with_memory_space_constraint(x, pltpu.HBM) for x in (cotangent, queries, documents)],
+        spaces=(pltpu.HBM,) * 3,
         scratch=(
+            pltpu.SMEM(cotangent.shape, F32),
             VMEM((n, width), BF16),
             VMEM((nd, width), BF16),
             VMEM((width + 16, nd), BF16),
             VMEM((nd, cols), F32),
-            pltpu.SemaphoreType.DMA((nb + 1,)),
+            pltpu.SemaphoreType.DMA((nb + 2,)),
         ),
         limit=16 << 20,
     )
     other_lse, other = swap(lse, "tok", 1), swap(odd, "tok", 1)
-    pair, own_q, *send_q = call(
-        pair_kernel,
-        "pair",
-        (stat, sds((width, blk), F32)) + (sds((width, blk), BF16),) * (chips - 1),
-        (even, other, lse, other_lse),
-    )
+    (pair,) = call(pair_kernel, "pair", (stat,), (lse, other_lse))
     far = [swap(pair, "tok", 2 * k) for k in range(1, chips)]
+    own_q, *send_q = call(
+        mean_kernel,
+        "mean",
+        (sds((width, blk), F32),) + (sds((width, blk), BF16),) * (chips - 1),
+        (even, other, lse, other_lse, pair),
+    )
     got_q = [swap(x, "tok", 2 * (k + 1)) for k, x in enumerate(send_q)]
-    share, own_d, *send_d = call(
+    e, qt = (pltpu.with_memory_space_constraint(x, VMEM) for x in (e, qt))
+    share, fq, *send_d = call(
         functools.partial(docs_kernel, chips),
         "docs",
-        (sds((chips, 1, blk), F32), sds((sub, width), F32)) + (sds((sub, width), BF16),) * (n_row - 1),
-        (
-            pltpu.with_memory_space_constraint(e, VMEM),
-            pltpu.with_memory_space_constraint(qt, VMEM),
-            top,
-            weight,
-            pair,
-            *far,
-        ),
-        scratch=(VMEM((groups, 2 * width, cols), BF16),),
+        (sds((chips, 1, blk), F32), VMEM((groups, 2 * width, cols), BF16)) + (sds((sub, width), BF16),) * (n_row - 1),
+        (e, qt, top, weight, own_q, pair, *far),
+        cost=pl.CostEstimate(flops=40 * nd * n * width, bytes_accessed=1 << 20, transcendentals=0),
     )
     got_d = [swap(x, "query", j + 1) for j, x in enumerate(send_d)]
+    (own_d,) = call(
+        own_docs_kernel,
+        "own",
+        (sds((sub, width), F32),),
+        (e, pltpu.with_memory_space_constraint(fq, VMEM)),
+        cost=pl.CostEstimate(flops=4 * sub * n * width, bytes_accessed=1 << 20, transcendentals=0),
+    )
     (grad_q,) = call(query_kernel, "queries", (sds((blk, width), F32),), (share, own_q, *got_q))
     grad_d = own_d
     for x in got_d:

time: 58 us -> 51.5 us (0.89)
  waiting for transfers between devices: 10 us -> 4.91 us
  local copies, waits for them, and re-layouts: 0.65 us -> 0 us
    ppermute x11, waiting for transfers between devices: 10 us -> 4.91 us  [swap(): lax.ppermute(x, axis, [(i, i ^ step) for i in range(lax.axis_size(axis))])]
    unnamed x2 -> x0, local copies, waits for them, and re-layouts: 0.65 us -> none
    pallas_call x4 -> x6, Pallas kernels: 30.9 us -> 30.5 us  [call(): pl.pallas_call(kernel, out_shape=tuple(outs), in_specs=[pl.BlockSpec(memo...]
  transfers between devices with their start and end apart: 11 -> 11, of which waited for: 6 -> 3; matrix products, arithmetic and copies ran while one was open for 0% -> 0% of each run, Pallas kernels for 9% -> 11%
where the time goes in v3:
time: 51.5 us; the launch traced here: 51.4 us
  Pallas kernels  30.5 us (59%)
  starting transfers between devices  14.6 us (28%)
  waiting for transfers between devices  4.91 us (10%)
  other arithmetic  0.76 us (1%)
  between operations  0.67 us (1%)
    pallas_call x6, Pallas kernels, call(): pl.pallas_call(kernel, out_shape=tuple(outs), in_specs=[pl.BlockSpec(memo...  30.5 us
    ppermute x11, starting transfers between devices, swap(): lax.ppermute(x, axis, [(i, i ^ step) for i in range(lax.axis_size(axis))])  14.6 us
    ppermute x11, waiting for transfers between devices, swap(): lax.ppermute(x, axis, [(i, i ^ step) for i in range(lax.axis_size(axis))])  4.91 us
  transfers between devices with their start and end apart: 11, of which 3 were waited for; matrix products, arithmetic and copies ran while one was open for 0% of the time, Pallas kernels for 11%

profile of v3, /device:TPU:0, one launch (start us, length us, event | category | flops | bytes accessed | tf_op | source)
XLA Modules:
  0.0 51.4 jit_solution(14339993902022755889)
XLA Ops:
  0.6 24.7 %tile.1 = (bf16[4,2048,1024]{2,1,0:T(8,128)(2,1)S(1)}, bf16[4,128,1024]{2,1,0:T(8,128)(2,1)S(1)}, f32[4,1,1024]{2,1,0:T(1,128)S(1)}, f32[2,128,1024]{2,1,0:T(8,1...) custom-call(f32[128]{0:T(128)} %cot_hbm.1, ...), custom_call_target="tpu_custom_call" | custom-call | tf_op jit(solution)/shard_map/tile/pallas_call | solution.py:203
  25.3 0.5 %collective-permute-start = (bf16[2,128,1024]{2,1,0:T(8,128)(2,1)S(1)}, bf16[2,128,1024]{2,1,0:T(8,128)(2,1)S(1)}, u32[]{:S(2)}, u32[]{:S(2)}) collective-permute-start(bf16[2,128,1024]{2,1,0:T(8,128)(2,1)S(1)} %get-tuple-element.23), channel_id=1, source_target_pairs={{0,1},{1,0},{2,3},{3,2},{4,5},{5,4},{6,7},{7,6},{8,9},{9,8},{10,11... | collective-permute-start | bytes 1572872 | tf_op jit(solution)/shard_map/ppermute | solution.py:216
  25.8 0.1 collective-permute-start.1
  25.9 1.5 %collective-permute-done.1.other_lse_ref = f32[4,1,1024]{2,1,0:T(1,128)S(1)} collective-permute-done((f32[4,1,1024]{2,1,0:T(1,128)S(1)}, f32[4,1,1024]{2,1,0:T(1,128)S(1)}, u32[]{:S(2)}, u32[]{:S(2)}) %collective-permute-start.1) | collective-permute-done | bytes 16416 | tf_op jit(solution)/shard_map/ppermute | solution.py:216
  27.4 5.0 %collective-permute-start.4 = (f32[4,1,1024]{2,1,0:T(1,128)S(1)}, f32[4,1,1024]{2,1,0:T(1,128)S(1)}, u32[]{:S(2)}, u32[]{:S(2)}) collective-permute-start(f32[4,1,1024]{2,1,0:T(1,128)S(1)} %pair.1.pair_ref), channel_id=1, source_target_pairs={{0,6},{1,7},{2,4},{3,5},{4,2},{5,3},{6,0},{7,1},{8,14},{9,15},{10,... | collective-permute-start | bytes 49160 | tf_op jit(solution)/shard_map/ppermute | solution.py:216
  32.4 0.0 collective-permute-start.3
  32.4 0.6 %collective-permute-start.2 = (f32[4,1,1024]{2,1,0:T(1,128)S(1)}, f32[4,1,1024]{2,1,0:T(1,128)S(1)}, u32[]{:S(2)}, u32[]{:S(2)}) collective-permute-start(f32[4,1,1024]{2,1,0:T(1,128)S(1)} %pair.1.pair_ref), channel_id=1, source_target_pairs={{0,2},{1,3},{2,0},{3,1},{4,6},{5,7},{6,4},{7,5},{8,10},{9,11},{10,... | collective-permute-start | bytes 49160 | tf_op jit(solution)/shard_map/ppermute | solution.py:216
  33.1 0.0 collective-permute-done.other_ref
  33.1 0.2 mean.1
  33.3 1.5 %collective-permute-start.5 = (bf16[128,512]{1,0:T(8,128)(2,1)S(1)}, bf16[128,512]{1,0:T(8,128)(2,1)S(1)}, u32[]{:S(2)}, u32[]{:S(2)}) collective-permute-start(bf16[128,512]{1,0:T(8,128)(2,1)S(1)} %get-tuple-element.27), channel_id=1, source_target_pairs={{0,2},{1,3},{2,0},{3,1},{4,6},{5,7},{6,4},{7,5},{8,10},{9,11},{10,... | collective-permute-start | bytes 393224 | tf_op jit(solution)/shard_map/ppermute | solution.py:216
  34.7 2.9 %collective-permute-start.6 = (bf16[128,512]{1,0:T(8,128)(2,1)S(1)}, bf16[128,512]{1,0:T(8,128)(2,1)S(1)}, u32[]{:S(2)}, u32[]{:S(2)}) collective-permute-start(bf16[128,512]{1,0:T(8,128)(2,1)S(1)} %get-tuple-element.28), channel_id=1, source_target_pairs={{0,4},{1,5},{2,6},{3,7},{4,0},{5,1},{6,2},{7,3},{8,12},{9,13},{10,... | collective-permute-start | bytes 393224 | tf_op jit(solution)/shard_map/ppermute | solution.py:216
  37.6 0.0 collective-permute-done.4.refs_2_
  37.6 0.3 collective-permute-start.7
  38.0 0.0 collective-permute-done.3.refs_1_
  38.0 0.0 collective-permute-done.2.refs_0_
  38.0 3.5 %docs.1 = (f32[4,1,512]{2,1,0:T(1,128)S(1)}, bf16[4,256,1024]{2,1,0:T(8,128)(2,1)S(1)}, bf16[512,128]{1,0:T(8,128)(2,1)S(1)}, bf16[512,128]{1,0:T(8,128)(2,1)S(1)}, bf16[512,128]{1,0:T(8,128)(2,1)S(1)}) custom-call(bf16[4,2048,1024]{2,1,0:T(8,128)(2,1)S(1)} %get-tuple-element.18.e_ref, bf16[4,128,1024]{2,1,0:T(8,128)(2,1)S(1)} %get-tuple-element.19.qt_ref, ...), custom_call_target="tpu_custom_call" | custom-call | flops 42949672960 | bytes 1048576 | tf_op jit(solution)/shard_map/docs/pallas_call | solution.py:203
  41.5 1.6 %collective-permute-start.8 = (bf16[512,128]{1,0:T(8,128)(2,1)S(1)}, bf16[512,128]{1,0:T(8,128)(2,1)S(1)}, u32[]{:S(2)}, u32[]{:S(2)}) collective-permute-start(bf16[512,128]{1,0:T(8,128)(2,1)S(1)} %get-tuple-element.31), channel_id=1, source_target_pairs={{0,8},{8,0},{16,24},{24,16},{1,9},{9,1},{17,25},{25,17},{2,10},{10... | collective-permute-start | bytes 393224 | tf_op jit(solution)/shard_map/ppermute | solution.py:216
  43.0 1.5 %collective-permute-start.9 = (bf16[512,128]{1,0:T(8,128)(2,1)S(1)}, bf16[512,128]{1,0:T(8,128)(2,1)S(1)}, u32[]{:S(2)}, u32[]{:S(2)}) collective-permute-start(bf16[512,128]{1,0:T(8,128)(2,1)S(1)} %get-tuple-element.32), channel_id=1, source_target_pairs={{0,16},{8,24},{16,0},{24,8},{1,17},{9,25},{17,1},{25,9},{2,18},{10... | collective-permute-start | bytes 393224 | tf_op jit(solution)/shard_map/ppermute | solution.py:216
  44.6 0.0 collective-permute-done.5.refs_0_
  44.6 0.5 collective-permute-start.10
  45.0 1.3 %own.1 = f32[512,128]{1,0:T(8,128)S(1)} custom-call(bf16[4,2048,1024]{2,1,0:T(8,128)(2,1)S(1)} %get-tuple-element.18.e_ref, bf16[4,256,1024]{2,1,0:T(8,128)(2,1)S(1)} %get-tuple-element.30.fq_ref), custom_call_target="tpu_custom_call" | custom-call | flops 1073741824 | bytes 1048576 | tf_op jit(solution)/shard_map/own/pallas_call | solution.py:203
  46.3 1.0 %collective-permute-done.6.refs_1_ = bf16[128,512]{1,0:T(8,128)(2,1)S(1)} collective-permute-done((bf16[128,512]{1,0:T(8,128)(2,1)S(1)}, bf16[128,512]{1,0:T(8,128)(2,1)S(1)}, u32[]{:S(2)}, u32[]{:S(2)}) %collective-permute-start.6) | collective-permute-done | bytes 131104 | tf_op jit(solution)/shard_map/ppermute | solution.py:216
  47.3 0.0 collective-permute-done.7.refs_2_
  47.3 0.9 %queries.1 = f32[512,128]{1,0:T(8,128)} custom-call(f32[4,1,512]{2,1,0:T(1,128)S(1)} %get-tuple-element.26.share_ref, f32[128,512]{1,0:T(8,128)S(1)} %get-tuple-element.25.gate_ref.own_ref, bf16[128,512]{1,0:T(8,128)(2,1)S(1)} %collective-permute-done.5.refs_0_, bf16[128,512]{1,0:T(8,128)(2,1)S(1)} %collective-permute-done.6.refs_1_, ...), custom_call_target="tpu_custom_call" | custom-call | tf_op jit(solution)/shard_map/queries/pallas_call | solution.py:203
  48.2 0.0 collective-permute-done.8
  48.2 2.4 %collective-permute-done.9 = bf16[512,128]{1,0:T(8,128)(2,1)S(1)} collective-permute-done((bf16[512,128]{1,0:T(8,128)(2,1)S(1)}, bf16[512,128]{1,0:T(8,128)(2,1)S(1)}, u32[]{:S(2)}, u32[]{:S(2)}) %collective-permute-start.9) | collective-permute-done | bytes 131104 | tf_op jit(solution)/shard_map/ppermute | solution.py:216
  50.6 0.0 collective-permute-done.10
  50.6 0.8 %add_bitcast_fusion = f32[1,512,128]{2,1,0:T(8,128)} fusion(bf16[512,128]{1,0:T(8,128)(2,1)S(1)} %collective-permute-done.10, bf16[512,128]{1,0:T(8,128)(2,1)S(1)} %collective-permute-done.9, f32[512,128]{1,0:T(8,128)S(1)} %own.1, bf16[512,128]{1,0:T(8,128)(2,1)S(1)} %collective-permute-done.8), kind=kLoop, calls=%fused_computation | loop fusion | flops 393216 | bytes 917504 | tf_op jit(solution)/shard_map/broadcast_in_dim | solution.py:284
  (1 shorter events, 0.0 us)
Async XLA Ops:
  25.3 7.8 %collective-permute-start = (bf16[2,128,1024]{2,1,0:T(8,128)(2,1)S(1)}, bf16[2,128,1024]{2,1,0:T(8,128)(2,1)S(1)}, u32[]{:S(2)}, u32[]{:S(2)}) collective-permute-start(bf16[2,128,1024]{2,1,0:T(8,128)(2,1)S(1)} %get-tuple-element.23), channel_id=1, source_target_pairs={{0,1},{1,0},{2,3},{3,2},{4,5},{5,4},{6,7},{7,6},{8,9},{9,8},{10,11... | collective-permute-start | bytes 1572872 | tf_op jit(solution)/shard_map/ppermute | solution.py:216
  25.8 1.6 %collective-permute-start.1 = (f32[4,1,1024]{2,1,0:T(1,128)S(1)}, f32[4,1,1024]{2,1,0:T(1,128)S(1)}, u32[]{:S(2)}, u32[]{:S(2)}) collective-permute-start(f32[4,1,1024]{2,1,0:T(1,128)S(1)} %get-tuple-element.24.lse_ref), channel_id=1, source_target_pairs={{0,1},{1,0},{2,3},{3,2},{4,5},{5,4},{6,7},{7,6},{8,9},{9,8},{10,11... | collective-permute-start | bytes 49160 | tf_op jit(solution)/shard_map/ppermute | solution.py:216
  27.4 10.2 %collective-permute-start.4 = (f32[4,1,1024]{2,1,0:T(1,128)S(1)}, f32[4,1,1024]{2,1,0:T(1,128)S(1)}, u32[]{:S(2)}, u32[]{:S(2)}) collective-permute-start(f32[4,1,1024]{2,1,0:T(1,128)S(1)} %pair.1.pair_ref), channel_id=1, source_target_pairs={{0,6},{1,7},{2,4},{3,5},{4,2},{5,3},{6,0},{7,1},{8,14},{9,15},{10,... | collective-permute-start | bytes 49160 | tf_op jit(solution)/shard_map/ppermute | solution.py:216
  32.4 5.5 %collective-permute-start.3 = (f32[4,1,1024]{2,1,0:T(1,128)S(1)}, f32[4,1,1024]{2,1,0:T(1,128)S(1)}, u32[]{:S(2)}, u32[]{:S(2)}) collective-permute-start(f32[4,1,1024]{2,1,0:T(1,128)S(1)} %pair.1.pair_ref), channel_id=1, source_target_pairs={{0,4},{1,5},{2,6},{3,7},{4,0},{5,1},{6,2},{7,3},{8,12},{9,13},{10,... | collective-permute-start | bytes 49160 | tf_op jit(solution)/shard_map/ppermute | solution.py:216
  32.4 5.5 %collective-permute-start.2 = (f32[4,1,1024]{2,1,0:T(1,128)S(1)}, f32[4,1,1024]{2,1,0:T(1,128)S(1)}, u32[]{:S(2)}, u32[]{:S(2)}) collective-permute-start(f32[4,1,1024]{2,1,0:T(1,128)S(1)} %pair.1.pair_ref), channel_id=1, source_target_pairs={{0,2},{1,3},{2,0},{3,1},{4,6},{5,7},{6,4},{7,5},{8,10},{9,11},{10,... | collective-permute-start | bytes 49160 | tf_op jit(solution)/shard_map/ppermute | solution.py:216
  33.3 11.3 %collective-permute-start.5 = (bf16[128,512]{1,0:T(8,128)(2,1)S(1)}, bf16[128,512]{1,0:T(8,128)(2,1)S(1)}, u32[]{:S(2)}, u32[]{:S(2)}) collective-permute-start(bf16[128,512]{1,0:T(8,128)(2,1)S(1)} %get-tuple-element.27), channel_id=1, source_target_pairs={{0,2},{1,3},{2,0},{3,1},{4,6},{5,7},{6,4},{7,5},{8,10},{9,11},{10,... | collective-permute-start | bytes 393224 | tf_op jit(solution)/shard_map/ppermute | solution.py:216
  34.7 12.6 %collective-permute-start.6 = (bf16[128,512]{1,0:T(8,128)(2,1)S(1)}, bf16[128,512]{1,0:T(8,128)(2,1)S(1)}, u32[]{:S(2)}, u32[]{:S(2)}) collective-permute-start(bf16[128,512]{1,0:T(8,128)(2,1)S(1)} %get-tuple-element.28), channel_id=1, source_target_pairs={{0,4},{1,5},{2,6},{3,7},{4,0},{5,1},{6,2},{7,3},{8,12},{9,13},{10,... | collective-permute-start | bytes 393224 | tf_op jit(solution)/shard_map/ppermute | solution.py:216
  37.6 9.7 %collective-permute-start.7 = (bf16[128,512]{1,0:T(8,128)(2,1)S(1)}, bf16[128,512]{1,0:T(8,128)(2,1)S(1)}, u32[]{:S(2)}, u32[]{:S(2)}) collective-permute-start(bf16[128,512]{1,0:T(8,128)(2,1)S(1)} %get-tuple-element.29), channel_id=1, source_target_pairs={{0,6},{1,7},{2,4},{3,5},{4,2},{5,3},{6,0},{7,1},{8,14},{9,15},{10,... | collective-permute-start | bytes 393224 | tf_op jit(solution)/shard_map/ppermute | solution.py:216
  41.5 6.7 %collective-permute-start.8 = (bf16[512,128]{1,0:T(8,128)(2,1)S(1)}, bf16[512,128]{1,0:T(8,128)(2,1)S(1)}, u32[]{:S(2)}, u32[]{:S(2)}) collective-permute-start(bf16[512,128]{1,0:T(8,128)(2,1)S(1)} %get-tuple-element.31), channel_id=1, source_target_pairs={{0,8},{8,0},{16,24},{24,16},{1,9},{9,1},{17,25},{25,17},{2,10},{10... | collective-permute-start | bytes 393224 | tf_op jit(solution)/shard_map/ppermute | solution.py:216
  43.0 7.6 %collective-permute-start.9 = (bf16[512,128]{1,0:T(8,128)(2,1)S(1)}, bf16[512,128]{1,0:T(8,128)(2,1)S(1)}, u32[]{:S(2)}, u32[]{:S(2)}) collective-permute-start(bf16[512,128]{1,0:T(8,128)(2,1)S(1)} %get-tuple-element.32), channel_id=1, source_target_pairs={{0,16},{8,24},{16,0},{24,8},{1,17},{9,25},{17,1},{25,9},{2,18},{10... | collective-permute-start | bytes 393224 | tf_op jit(solution)/shard_map/ppermute | solution.py:216
  44.6 6.1 %collective-permute-start.10 = (bf16[512,128]{1,0:T(8,128)(2,1)S(1)}, bf16[512,128]{1,0:T(8,128)(2,1)S(1)}, u32[]{:S(2)}, u32[]{:S(2)}) collective-permute-start(bf16[512,128]{1,0:T(8,128)(2,1)S(1)} %get-tuple-element.33), channel_id=1, source_target_pairs={{0,24},{8,16},{16,8},{24,0},{1,25},{9,17},{17,9},{25,1},{2,26},{10... | collective-permute-start | bytes 393224 | tf_op jit(solution)/shard_map/ppermute | solution.py:216

commit v4 on v3

--- a/solution.py
+++ b/solution.py
@@ -57,7 +57,11 @@
     copies.append(pltpu.make_async_copy(cot_hbm, cot_ref, sems.at[nb + 1]))
     for copy in copies:
         copy.start()
-    for copy in copies:
+    copies[0].wait()
+    dt_ref[:width, :] = d_ref[...].T
+    extra = (dt_ref.shape[0] - width, nd)
+    dt_ref[width:, :] = jnp.where(lax.broadcasted_iota(jnp.int32, extra, 0) == 0, 1.0, 0.0).astype(BF16)
+    for copy in copies[1:]:
         copy.wait()
 
     query = lax.broadcasted_iota(jnp.int32, (1, blk), 1) // QLEN
@@ -69,46 +73,33 @@
         group, lane = divmod(slot * blk, cols)
         weight_ref[group, :, lane : lane + blk] = row
 
-    dt_ref[:width, :] = d_ref[...].T
-    extra = (dt_ref.shape[0] - width, nd)
-    dt_ref[width:, :] = jnp.where(lax.broadcasted_iota(jnp.int32, extra, 0) == 0, 1.0, 0.0).astype(BF16)
-
+    def finish(g, total):
+        mass = total[width : width + 1, :]
+        mean = total[:width, :] * (1.0 / mass)
+        if g < groups // 2:
+            odd_ref[g] = mean.astype(BF16)
+        else:
+            even_ref[g - groups // 2] = mean
+        spread = jnp.log2(mass)
+        lse_ref[g] = top_ref[g] + spread
+        return spread
+
+    for g in range(groups):
+        top_ref[g] = column_max(nt_dot(d_ref[:sample, :], q_ref[g * cols : (g + 1) * cols, :])) * SCALE
+    spread = jnp.zeros((1, cols), F32)
     for g in range(groups):
         rows = q_ref[g * cols : (g + 1) * cols, :]
         qt_ref[g] = rows.T
-        top_ref[g] = column_max(nt_dot(d_ref[:sample, :], rows)) * SCALE
-
-    def finish(g):
-        total = nn_dot(dt_ref[...], e_ref[g])
-        mass = total[width : width + 1, :]
-        mean = total[:width, :] * (1.0 / mass)
-
-        @pl.when(g < groups // 2)
-        def _():
-            odd_ref[g] = mean.astype(BF16)
-
-        @pl.when(g >= groups // 2)
-        def _():
-            even_ref[g - groups // 2] = mean
-
-        spread = jnp.log2(mass)
-        lse_ref[g] = top_ref[g] + spread
-        return spread
-
-    def quick(g, carry):
-        rows = q_ref[pl.ds(pl.multiple_of(g * cols, cols), cols), :]
         top = top_ref[g]
         for at in range(0, nd, step):
             s = nt_dot(d_ref[at : at + step, :], rows)
             e_ref[g, at : at + step, :] = jnp.exp2(s * SCALE - top).astype(BF16)
-        return jnp.maximum(carry, finish(g))
-
-    spread = lax.fori_loop(0, groups, quick, jnp.zeros((1, cols), F32))
+        spread = jnp.maximum(spread, finish(g, nn_dot(dt_ref[...], e_ref[g])))
 
     @pl.when(jnp.logical_not(jnp.max(spread) <= ROOM))
     def _():
-        def careful(g, carry):
-            rows = q_ref[pl.ds(pl.multiple_of(g * cols, cols), cols), :]
+        for g in range(groups):
+            rows = q_ref[g * cols : (g + 1) * cols, :]
             top = None
             for at in range(0, nd, step):
                 s = nt_dot(d_ref[at : at + step, :], rows)
@@ -119,10 +110,7 @@
             top_ref[g] = top
             for at in range(0, nd, step):
                 e_ref[g, at : at + step, :] = jnp.exp2(s_ref[at : at + step, :] * SCALE - top).astype(BF16)
-            finish(g)
-            return carry
-
-        lax.fori_loop(0, groups, careful, 0)
+            finish(g, nn_dot(dt_ref[...], e_ref[g]))
 
 
 def pair_kernel(lse_ref, other_lse_ref, pair_ref):
@@ -279,7 +267,7 @@
     )
     (grad_q,) = call(query_kernel, "queries", (sds((blk, width), F32),), (share, own_q, *got_q))
     grad_d = own_d
-    for x in got_d:
+    for x in reversed(got_d):
         grad_d = grad_d + x.astype(F32)
     return grad_q, grad_d[None]
 

time: 51.5 us -> 48.7 us (0.946)
  Pallas kernels: 30.5 us -> 28.8 us
  waiting for transfers between devices: 4.91 us -> 3.79 us
    pallas_call x6, Pallas kernels: 30.5 us -> 28.8 us  [call(): pl.pallas_call(kernel, out_shape=tuple(outs), in_specs=[pl.BlockSpec(memo...]
    ppermute x11, waiting for transfers between devices: 4.91 us -> 3.79 us  [swap(): lax.ppermute(x, axis, [(i, i ^ step) for i in range(lax.axis_size(axis))])]
  transfers between devices with their start and end apart: 11 -> 11, of which waited for: 3 -> 4; matrix products, arithmetic and copies ran while one was open for 0% -> 0% of each run, Pallas kernels for 11% -> 12%
where the time goes in v4:
time: 48.7 us; the launch traced here: 48.5 us
  Pallas kernels  28.8 us (59%)
  starting transfers between devices  14.6 us (30%)
  waiting for transfers between devices  3.79 us (8%)
  other arithmetic  0.76 us (2%)
  between operations  0.67 us (1%)
    pallas_call x6, Pallas kernels, call(): pl.pallas_call(kernel, out_shape=tuple(outs), in_specs=[pl.BlockSpec(memo...  28.8 us
    ppermute x11, starting transfers between devices, swap(): lax.ppermute(x, axis, [(i, i ^ step) for i in range(lax.axis_size(axis))])  14.6 us
    ppermute x11, waiting for transfers between devices, swap(): lax.ppermute(x, axis, [(i, i ^ step) for i in range(lax.axis_size(axis))])  3.79 us
  transfers between devices with their start and end apart: 11, of which 4 were waited for; matrix products, arithmetic and copies ran while one was open for 0% of the time, Pallas kernels for 12%

profile of v4, /device:TPU:0, one launch (start us, length us, event | category | flops | bytes accessed | tf_op | source)
XLA Modules:
  0.0 48.5 jit_solution(8539211317620575103)
XLA Ops:
  0.6 22.9 %tile.1 = (bf16[4,2048,1024]{2,1,0:T(8,128)(2,1)S(1)}, bf16[4,128,1024]{2,1,0:T(8,128)(2,1)S(1)}, f32[4,1,1024]{2,1,0:T(1,128)S(1)}, f32[2,128,1024]{2,1,0:T(8,1...) custom-call(f32[128]{0:T(128)} %cot_hbm.1, ...), custom_call_target="tpu_custom_call" | custom-call | tf_op jit(solution)/shard_map/tile/pallas_call | solution.py:191
  23.6 0.5 %collective-permute-start = (bf16[2,128,1024]{2,1,0:T(8,128)(2,1)S(1)}, bf16[2,128,1024]{2,1,0:T(8,128)(2,1)S(1)}, u32[]{:S(2)}, u32[]{:S(2)}) collective-permute-start(bf16[2,128,1024]{2,1,0:T(8,128)(2,1)S(1)} %get-tuple-element.23), channel_id=1, source_target_pairs={{0,1},{1,0},{2,3},{3,2},{4,5},{5,4},{6,7},{7,6},{8,9},{9,8},{10,11... | collective-permute-start | bytes 1572872 | tf_op jit(solution)/shard_map/ppermute | solution.py:204
  24.1 0.1 collective-permute-start.1
  24.2 1.5 %collective-permute-done.1.other_lse_ref = f32[4,1,1024]{2,1,0:T(1,128)S(1)} collective-permute-done((f32[4,1,1024]{2,1,0:T(1,128)S(1)}, f32[4,1,1024]{2,1,0:T(1,128)S(1)}, u32[]{:S(2)}, u32[]{:S(2)}) %collective-permute-start.1) | collective-permute-done | bytes 16416 | tf_op jit(solution)/shard_map/ppermute | solution.py:204
  25.7 5.0 %collective-permute-start.4 = (f32[4,1,1024]{2,1,0:T(1,128)S(1)}, f32[4,1,1024]{2,1,0:T(1,128)S(1)}, u32[]{:S(2)}, u32[]{:S(2)}) collective-permute-start(f32[4,1,1024]{2,1,0:T(1,128)S(1)} %pair.1.pair_ref), channel_id=1, source_target_pairs={{0,6},{1,7},{2,4},{3,5},{4,2},{5,3},{6,0},{7,1},{8,14},{9,15},{10,... | collective-permute-start | bytes 49160 | tf_op jit(solution)/shard_map/ppermute | solution.py:204
  30.7 0.0 collective-permute-start.3
  30.7 0.6 %collective-permute-start.2 = (f32[4,1,1024]{2,1,0:T(1,128)S(1)}, f32[4,1,1024]{2,1,0:T(1,128)S(1)}, u32[]{:S(2)}, u32[]{:S(2)}) collective-permute-start(f32[4,1,1024]{2,1,0:T(1,128)S(1)} %pair.1.pair_ref), channel_id=1, source_target_pairs={{0,2},{1,3},{2,0},{3,1},{4,6},{5,7},{6,4},{7,5},{8,10},{9,11},{10,... | collective-permute-start | bytes 49160 | tf_op jit(solution)/shard_map/ppermute | solution.py:204
  31.4 0.0 collective-permute-done.other_ref
  31.4 0.2 mean.1
  31.5 1.5 %collective-permute-start.5 = (bf16[128,512]{1,0:T(8,128)(2,1)S(1)}, bf16[128,512]{1,0:T(8,128)(2,1)S(1)}, u32[]{:S(2)}, u32[]{:S(2)}) collective-permute-start(bf16[128,512]{1,0:T(8,128)(2,1)S(1)} %get-tuple-element.27), channel_id=1, source_target_pairs={{0,2},{1,3},{2,0},{3,1},{4,6},{5,7},{6,4},{7,5},{8,10},{9,11},{10,... | collective-permute-start | bytes 393224 | tf_op jit(solution)/shard_map/ppermute | solution.py:204
  33.0 2.9 %collective-permute-start.6 = (bf16[128,512]{1,0:T(8,128)(2,1)S(1)}, bf16[128,512]{1,0:T(8,128)(2,1)S(1)}, u32[]{:S(2)}, u32[]{:S(2)}) collective-permute-start(bf16[128,512]{1,0:T(8,128)(2,1)S(1)} %get-tuple-element.28), channel_id=1, source_target_pairs={{0,4},{1,5},{2,6},{3,7},{4,0},{5,1},{6,2},{7,3},{8,12},{9,13},{10,... | collective-permute-start | bytes 393224 | tf_op jit(solution)/shard_map/ppermute | solution.py:204
  35.9 0.0 collective-permute-done.4.refs_2_
  35.9 0.3 collective-permute-start.7
  36.3 0.0 collective-permute-done.3.refs_1_
  36.3 0.0 collective-permute-done.2.refs_0_
  36.3 3.5 %docs.1 = (f32[4,1,512]{2,1,0:T(1,128)S(1)}, bf16[4,256,1024]{2,1,0:T(8,128)(2,1)S(1)}, bf16[512,128]{1,0:T(8,128)(2,1)S(1)}, bf16[512,128]{1,0:T(8,128)(2,1)S(1)}, bf16[512,128]{1,0:T(8,128)(2,1)S(1)}) custom-call(bf16[4,2048,1024]{2,1,0:T(8,128)(2,1)S(1)} %get-tuple-element.18.e_ref, bf16[4,128,1024]{2,1,0:T(8,128)(2,1)S(1)} %get-tuple-element.19.qt_ref, ...), custom_call_target="tpu_custom_call" | custom-call | flops 42949672960 | bytes 1048576 | tf_op jit(solution)/shard_map/docs/pallas_call | solution.py:191
  39.8 2.5 %collective-permute-start.8 = (bf16[512,128]{1,0:T(8,128)(2,1)S(1)}, bf16[512,128]{1,0:T(8,128)(2,1)S(1)}, u32[]{:S(2)}, u32[]{:S(2)}) collective-permute-start(bf16[512,128]{1,0:T(8,128)(2,1)S(1)} %get-tuple-element.31), channel_id=1, source_target_pairs={{0,24},{8,16},{16,8},{24,0},{1,25},{9,17},{17,9},{25,1},{2,26},{10... | collective-permute-start | bytes 393224 | tf_op jit(solution)/shard_map/ppermute | solution.py:204
  42.3 0.5 %collective-permute-start.9 = (bf16[512,128]{1,0:T(8,128)(2,1)S(1)}, bf16[512,128]{1,0:T(8,128)(2,1)S(1)}, u32[]{:S(2)}, u32[]{:S(2)}) collective-permute-start(bf16[512,128]{1,0:T(8,128)(2,1)S(1)} %get-tuple-element.32), channel_id=1, source_target_pairs={{0,16},{8,24},{16,0},{24,8},{1,17},{9,25},{17,1},{25,9},{2,18},{10... | collective-permute-start | bytes 393224 | tf_op jit(solution)/shard_map/ppermute | solution.py:204
  42.8 0.0 collective-permute-done.5.refs_0_
  42.8 0.5 %collective-permute-start.10 = (bf16[512,128]{1,0:T(8,128)(2,1)S(1)}, bf16[512,128]{1,0:T(8,128)(2,1)S(1)}, u32[]{:S(2)}, u32[]{:S(2)}) collective-permute-start(bf16[512,128]{1,0:T(8,128)(2,1)S(1)} %get-tuple-element.33), channel_id=1, source_target_pairs={{0,8},{8,0},{16,24},{24,16},{1,9},{9,1},{17,25},{25,17},{2,10},{10... | collective-permute-start | bytes 393224 | tf_op jit(solution)/shard_map/ppermute | solution.py:204
  43.3 1.3 %own.1 = f32[512,128]{1,0:T(8,128)S(1)} custom-call(bf16[4,2048,1024]{2,1,0:T(8,128)(2,1)S(1)} %get-tuple-element.18.e_ref, bf16[4,256,1024]{2,1,0:T(8,128)(2,1)S(1)} %get-tuple-element.30.fq_ref), custom_call_target="tpu_custom_call" | custom-call | flops 1073741824 | bytes 1048576 | tf_op jit(solution)/shard_map/own/pallas_call | solution.py:191
  44.6 1.0 %collective-permute-done.6.refs_1_ = bf16[128,512]{1,0:T(8,128)(2,1)S(1)} collective-permute-done((bf16[128,512]{1,0:T(8,128)(2,1)S(1)}, bf16[128,512]{1,0:T(8,128)(2,1)S(1)}, u32[]{:S(2)}, u32[]{:S(2)}) %collective-permute-start.6) | collective-permute-done | bytes 131104 | tf_op jit(solution)/shard_map/ppermute | solution.py:204
  45.6 0.0 collective-permute-done.7.refs_2_
  45.6 0.9 %queries.1 = f32[512,128]{1,0:T(8,128)} custom-call(f32[4,1,512]{2,1,0:T(1,128)S(1)} %get-tuple-element.26.share_ref, f32[128,512]{1,0:T(8,128)S(1)} %get-tuple-element.25.gate_ref.own_ref, bf16[128,512]{1,0:T(8,128)(2,1)S(1)} %collective-permute-done.5.refs_0_, bf16[128,512]{1,0:T(8,128)(2,1)S(1)} %collective-permute-done.6.refs_1_, ...), custom_call_target="tpu_custom_call" | custom-call | tf_op jit(solution)/shard_map/queries/pallas_call | solution.py:191
  46.5 0.4 collective-permute-done.8
  46.9 0.9 %collective-permute-done.9 = bf16[512,128]{1,0:T(8,128)(2,1)S(1)} collective-permute-done((bf16[512,128]{1,0:T(8,128)(2,1)S(1)}, bf16[512,128]{1,0:T(8,128)(2,1)S(1)}, u32[]{:S(2)}, u32[]{:S(2)}) %collective-permute-start.9) | collective-permute-done | bytes 131104 | tf_op jit(solution)/shard_map/ppermute | solution.py:204
  47.8 0.0 collective-permute-done.10
  47.8 0.8 %add_bitcast_fusion = f32[1,512,128]{2,1,0:T(8,128)} fusion(bf16[512,128]{1,0:T(8,128)(2,1)S(1)} %collective-permute-done.10, bf16[512,128]{1,0:T(8,128)(2,1)S(1)} %collective-permute-done.9, f32[512,128]{1,0:T(8,128)S(1)} %own.1, bf16[512,128]{1,0:T(8,128)(2,1)S(1)} %collective-permute-done.8), kind=kLoop, calls=%fused_computation | loop fusion | flops 393216 | bytes 917504 | tf_op jit(solution)/shard_map/broadcast_in_dim | solution.py:272
  (1 shorter events, 0.0 us)
Async XLA Ops:
  23.6 7.8 %collective-permute-start = (bf16[2,128,1024]{2,1,0:T(8,128)(2,1)S(1)}, bf16[2,128,1024]{2,1,0:T(8,128)(2,1)S(1)}, u32[]{:S(2)}, u32[]{:S(2)}) collective-permute-start(bf16[2,128,1024]{2,1,0:T(8,128)(2,1)S(1)} %get-tuple-element.23), channel_id=1, source_target_pairs={{0,1},{1,0},{2,3},{3,2},{4,5},{5,4},{6,7},{7,6},{8,9},{9,8},{10,11... | collective-permute-start | bytes 1572872 | tf_op jit(solution)/shard_map/ppermute | solution.py:204
  24.1 1.6 %collective-permute-start.1 = (f32[4,1,1024]{2,1,0:T(1,128)S(1)}, f32[4,1,1024]{2,1,0:T(1,128)S(1)}, u32[]{:S(2)}, u32[]{:S(2)}) collective-permute-start(f32[4,1,1024]{2,1,0:T(1,128)S(1)} %get-tuple-element.24.lse_ref), channel_id=1, source_target_pairs={{0,1},{1,0},{2,3},{3,2},{4,5},{5,4},{6,7},{7,6},{8,9},{9,8},{10,11... | collective-permute-start | bytes 49160 | tf_op jit(solution)/shard_map/ppermute | solution.py:204
  25.7 10.2 %collective-permute-start.4 = (f32[4,1,1024]{2,1,0:T(1,128)S(1)}, f32[4,1,1024]{2,1,0:T(1,128)S(1)}, u32[]{:S(2)}, u32[]{:S(2)}) collective-permute-start(f32[4,1,1024]{2,1,0:T(1,128)S(1)} %pair.1.pair_ref), channel_id=1, source_target_pairs={{0,6},{1,7},{2,4},{3,5},{4,2},{5,3},{6,0},{7,1},{8,14},{9,15},{10,... | collective-permute-start | bytes 49160 | tf_op jit(solution)/shard_map/ppermute | solution.py:204
  30.7 5.5 %collective-permute-start.3 = (f32[4,1,1024]{2,1,0:T(1,128)S(1)}, f32[4,1,1024]{2,1,0:T(1,128)S(1)}, u32[]{:S(2)}, u32[]{:S(2)}) collective-permute-start(f32[4,1,1024]{2,1,0:T(1,128)S(1)} %pair.1.pair_ref), channel_id=1, source_target_pairs={{0,4},{1,5},{2,6},{3,7},{4,0},{5,1},{6,2},{7,3},{8,12},{9,13},{10,... | collective-permute-start | bytes 49160 | tf_op jit(solution)/shard_map/ppermute | solution.py:204
  30.7 5.5 %collective-permute-start.2 = (f32[4,1,1024]{2,1,0:T(1,128)S(1)}, f32[4,1,1024]{2,1,0:T(1,128)S(1)}, u32[]{:S(2)}, u32[]{:S(2)}) collective-permute-start(f32[4,1,1024]{2,1,0:T(1,128)S(1)} %pair.1.pair_ref), channel_id=1, source_target_pairs={{0,2},{1,3},{2,0},{3,1},{4,6},{5,7},{6,4},{7,5},{8,10},{9,11},{10,... | collective-permute-start | bytes 49160 | tf_op jit(solution)/shard_map/ppermute | solution.py:204
  31.5 11.3 %collective-permute-start.5 = (bf16[128,512]{1,0:T(8,128)(2,1)S(1)}, bf16[128,512]{1,0:T(8,128)(2,1)S(1)}, u32[]{:S(2)}, u32[]{:S(2)}) collective-permute-start(bf16[128,512]{1,0:T(8,128)(2,1)S(1)} %get-tuple-element.27), channel_id=1, source_target_pairs={{0,2},{1,3},{2,0},{3,1},{4,6},{5,7},{6,4},{7,5},{8,10},{9,11},{10,... | collective-permute-start | bytes 393224 | tf_op jit(solution)/shard_map/ppermute | solution.py:204
  33.0 12.6 %collective-permute-start.6 = (bf16[128,512]{1,0:T(8,128)(2,1)S(1)}, bf16[128,512]{1,0:T(8,128)(2,1)S(1)}, u32[]{:S(2)}, u32[]{:S(2)}) collective-permute-start(bf16[128,512]{1,0:T(8,128)(2,1)S(1)} %get-tuple-element.28), channel_id=1, source_target_pairs={{0,4},{1,5},{2,6},{3,7},{4,0},{5,1},{6,2},{7,3},{8,12},{9,13},{10,... | collective-permute-start | bytes 393224 | tf_op jit(solution)/shard_map/ppermute | solution.py:204
  35.9 9.7 %collective-permute-start.7 = (bf16[128,512]{1,0:T(8,128)(2,1)S(1)}, bf16[128,512]{1,0:T(8,128)(2,1)S(1)}, u32[]{:S(2)}, u32[]{:S(2)}) collective-permute-start(bf16[128,512]{1,0:T(8,128)(2,1)S(1)} %get-tuple-element.29), channel_id=1, source_target_pairs={{0,6},{1,7},{2,4},{3,5},{4,2},{5,3},{6,0},{7,1},{8,14},{9,15},{10,... | collective-permute-start | bytes 393224 | tf_op jit(solution)/shard_map/ppermute | solution.py:204
  39.8 7.2 %collective-permute-start.8 = (bf16[512,128]{1,0:T(8,128)(2,1)S(1)}, bf16[512,128]{1,0:T(8,128)(2,1)S(1)}, u32[]{:S(2)}, u32[]{:S(2)}) collective-permute-start(bf16[512,128]{1,0:T(8,128)(2,1)S(1)} %get-tuple-element.31), channel_id=1, source_target_pairs={{0,24},{8,16},{16,8},{24,0},{1,25},{9,17},{17,9},{25,1},{2,26},{10... | collective-permute-start | bytes 393224 | tf_op jit(solution)/shard_map/ppermute | solution.py:204
  42.3 5.5 %collective-permute-start.9 = (bf16[512,128]{1,0:T(8,128)(2,1)S(1)}, bf16[512,128]{1,0:T(8,128)(2,1)S(1)}, u32[]{:S(2)}, u32[]{:S(2)}) collective-permute-start(bf16[512,128]{1,0:T(8,128)(2,1)S(1)} %get-tuple-element.32), channel_id=1, source_target_pairs={{0,16},{8,24},{16,0},{24,8},{1,17},{9,25},{17,1},{25,9},{2,18},{10... | collective-permute-start | bytes 393224 | tf_op jit(solution)/shard_map/ppermute | solution.py:204
  42.8 5.0 %collective-permute-start.10 = (bf16[512,128]{1,0:T(8,128)(2,1)S(1)}, bf16[512,128]{1,0:T(8,128)(2,1)S(1)}, u32[]{:S(2)}, u32[]{:S(2)}) collective-permute-start(bf16[512,128]{1,0:T(8,128)(2,1)S(1)} %get-tuple-element.33), channel_id=1, source_target_pairs={{0,8},{8,0},{16,24},{24,16},{1,9},{9,1},{17,25},{25,17},{2,10},{10... | collective-permute-start | bytes 393224 | tf_op jit(solution)/shard_map/ppermute | solution.py:204

commit v5 on v4

--- a/solution.py
+++ b/solution.py
@@ -37,7 +37,7 @@
 
 
 def tile_kernel(
-    cot_hbm, q_hbm, d_hbm, e_ref, qt_ref, weight_ref, even_ref, odd_ref, lse_ref, top_ref, cot_ref, q_ref, d_ref, dt_ref, s_ref, sems
+    cot_hbm, q_hbm, d_hbm, e_ref, qt_ref, weight_ref, odd_ref, lse_ref, top_ref, dt_ref, cot_ref, q_ref, d_ref, s_ref, sems
 ):
     groups, nd, cols = e_ref.shape
     n, width = q_ref.shape
@@ -73,13 +73,13 @@
         group, lane = divmod(slot * blk, cols)
         weight_ref[group, :, lane : lane + blk] = row
 
-    def finish(g, total):
-        mass = total[width : width + 1, :]
-        mean = total[:width, :] * (1.0 / mass)
+    def finish(g, sums):
         if g < groups // 2:
-            odd_ref[g] = mean.astype(BF16)
+            total = nn_dot(dt_ref[...], e_ref[g])
+            mass = total[width : width + 1, :]
+            odd_ref[g] = (total[:width, :] * (1.0 / mass)).astype(BF16)
         else:
-            even_ref[g - groups // 2] = mean
+            mass = jnp.sum(sums, axis=0, keepdims=True)
         spread = jnp.log2(mass)
         lse_ref[g] = top_ref[g] + spread
         return spread
@@ -91,16 +91,21 @@
         rows = q_ref[g * cols : (g + 1) * cols, :]
         qt_ref[g] = rows.T
         top = top_ref[g]
+        sums = jnp.zeros((8, cols), F32)
         for at in range(0, nd, step):
             s = nt_dot(d_ref[at : at + step, :], rows)
-            e_ref[g, at : at + step, :] = jnp.exp2(s * SCALE - top).astype(BF16)
-        spread = jnp.maximum(spread, finish(g, nn_dot(dt_ref[...], e_ref[g])))
+            e = jnp.exp2(s * SCALE - top)
+            e_ref[g, at : at + step, :] = e.astype(BF16)
+            if g >= groups // 2:
+                sums = sums + jnp.sum(e.reshape(step // 8, 8, cols), axis=0)
+        spread = jnp.maximum(spread, finish(g, sums))
 
     @pl.when(jnp.logical_not(jnp.max(spread) <= ROOM))
     def _():
         for g in range(groups):
             rows = q_ref[g * cols : (g + 1) * cols, :]
             top = None
+            sums = jnp.zeros((8, cols), F32)
             for at in range(0, nd, step):
                 s = nt_dot(d_ref[at : at + step, :], rows)
                 s_ref[at : at + step, :] = s
@@ -109,11 +114,21 @@
             top = top * SCALE
             top_ref[g] = top
             for at in range(0, nd, step):
-                e_ref[g, at : at + step, :] = jnp.exp2(s_ref[at : at + step, :] * SCALE - top).astype(BF16)
-            finish(g, nn_dot(dt_ref[...], e_ref[g]))
-
-
-def pair_kernel(lse_ref, other_lse_ref, pair_ref):
+                e = jnp.exp2(s_ref[at : at + step, :] * SCALE - top)
+                e_ref[g, at : at + step, :] = e.astype(BF16)
+                sums = sums + jnp.sum(e.reshape(step // 8, 8, cols), axis=0)
+            finish(g, sums)
+
+
+def even_kernel(e_ref, dt_ref, lse_ref, top_ref, even_ref):
+    half, width, _ = even_ref.shape
+    for h in range(half):
+        total = nn_dot(dt_ref[:width, :], e_ref[half + h])
+        even_ref[h] = total * jnp.exp2(top_ref[half + h] - lse_ref[half + h])
+
+
+def pair_kernel(lse_ref, other_lse_ref, gate_ref, pair_ref):
+    del gate_ref
     groups = lse_ref.shape[0]
     for g in range(groups):
         pair_ref[g] = logsum2([lse_ref[g], other_lse_ref[(g + groups // 2) % groups]])
@@ -135,9 +150,13 @@
                 send_refs[k - 1][...] = part.astype(BF16)
 
 
+def far_order(chips):
+    return [0] + list(range(chips - 2, 0, -1))
+
+
 def docs_kernel(chips, e_ref, qt_ref, top_ref, weight_ref, gate_ref, pair_ref, *refs):
     del gate_ref
-    far = refs[: chips - 1]
+    far = [ref for _, ref in sorted(zip(far_order(chips), refs), key=lambda pair: pair[0])]
     share_ref, fq_ref = refs[chips - 1 : chips + 1]
     send_refs = refs[chips + 1 :]
     groups, nd, cols = e_ref.shape
@@ -215,17 +234,17 @@
     sds = jax.ShapeDtypeStruct
     stat = sds((groups, 1, cols), F32)
 
-    e, qt, weight, even, odd, lse, top = call(
+    e, qt, weight, odd, lse, top, dt = call(
         tile_kernel,
         "tile",
         (
             VMEM((groups, nd, cols), BF16),
             VMEM((groups, width, cols), BF16),
             stat,
-            sds((groups // 2, width, cols), F32),
             sds((groups // 2, width, cols), BF16),
             stat,
             stat,
+            VMEM((width + 16, nd), BF16),
         ),
         [pltpu.with_memory_space_constraint(x, pltpu.HBM) for x in (cotangent, queries, documents)],
         spaces=(pltpu.HBM,) * 3,
@@ -233,14 +252,21 @@
             pltpu.SMEM(cotangent.shape, F32),
             VMEM((n, width), BF16),
             VMEM((nd, width), BF16),
-            VMEM((width + 16, nd), BF16),
             VMEM((nd, cols), F32),
             pltpu.SemaphoreType.DMA((nb + 2,)),
         ),
         limit=16 << 20,
     )
     other_lse, other = swap(lse, "tok", 1), swap(odd, "tok", 1)
-    (pair,) = call(pair_kernel, "pair", (stat,), (lse, other_lse))
+    e, qt, dt = (pltpu.with_memory_space_constraint(x, VMEM) for x in (e, qt, dt))
+    (even,) = call(
+        even_kernel,
+        "even",
+        (sds((groups // 2, width, cols), F32),),
+        (e, dt, lse, top),
+        cost=pl.CostEstimate(flops=8 * nd * n * width, bytes_accessed=1 << 20, transcendentals=0),
+    )
+    (pair,) = call(pair_kernel, "pair", (stat,), (lse, other_lse, even))
     far = [swap(pair, "tok", 2 * k) for k in range(1, chips)]
     own_q, *send_q = call(
         mean_kernel,
@@ -249,12 +275,11 @@
         (even, other, lse, other_lse, pair),
     )
     got_q = [swap(x, "tok", 2 * (k + 1)) for k, x in enumerate(send_q)]
-    e, qt = (pltpu.with_memory_space_constraint(x, VMEM) for x in (e, qt))
     share, fq, *send_d = call(
         functools.partial(docs_kernel, chips),
         "docs",
         (sds((chips, 1, blk), F32), VMEM((groups, 2 * width, cols), BF16)) + (sds((sub, width), BF16),) * (n_row - 1),
-        (e, qt, top, weight, own_q, pair, *far),
+        (e, qt, top, weight, own_q, pair, *[far[i] for i in far_order(chips)]),
         cost=pl.CostEstimate(flops=40 * nd * n * width, bytes_accessed=1 << 20, transcendentals=0),
     )
     got_d = [swap(x, "query", j + 1) for j, x in enumerate(send_d)]

time: 48.7 us -> 45.8 us (0.940)
  waiting for transfers between devices: 3.79 us -> 2.34 us
  Pallas kernels: 28.8 us -> 27.6 us
    ppermute x11, waiting for transfers between devices: 3.79 us -> 2.34 us  [swap(): lax.ppermute(x, axis, [(i, i ^ step) for i in range(lax.axis_size(axis))])]
    pallas_call x6 -> x7, Pallas kernels: 28.8 us -> 27.6 us  [call(): pl.pallas_call(kernel, out_shape=tuple(outs), in_specs=[pl.BlockSpec(memo...]
  transfers between devices with their start and end apart: 11 -> 11, of which waited for: 4 -> 3; matrix products, arithmetic and copies ran while one was open for 0% -> 0% of each run, Pallas kernels for 12% -> 16%
where the time goes in v5:
time: 45.8 us; the launch traced here: 45.7 us
  Pallas kernels  27.6 us (60%)
  starting transfers between devices  14.3 us (31%)
  waiting for transfers between devices  2.34 us (5%)
  other arithmetic  0.77 us (2%)
  between operations  0.69 us (2%)
    pallas_call x7, Pallas kernels, call(): pl.pallas_call(kernel, out_shape=tuple(outs), in_specs=[pl.BlockSpec(memo...  27.6 us
    ppermute x11, starting transfers between devices, swap(): lax.ppermute(x, axis, [(i, i ^ step) for i in range(lax.axis_size(axis))])  14.3 us
    ppermute x11, waiting for transfers between devices, swap(): lax.ppermute(x, axis, [(i, i ^ step) for i in range(lax.axis_size(axis))])  2.34 us
  transfers between devices with their start and end apart: 11, of which 3 were waited for; matrix products, arithmetic and copies ran while one was open for 0% of the time, Pallas kernels for 16%

profile of v5, /device:TPU:0, one launch (start us, length us, event | category | flops | bytes accessed | tf_op | source)
XLA Modules:
  0.0 45.7 jit_solution(6449717032472983713)
XLA Ops:
  0.6 20.5 %tile.1 = (bf16[4,2048,1024]{2,1,0:T(8,128)(2,1)S(1)}, bf16[4,128,1024]{2,1,0:T(8,128)(2,1)S(1)}, f32[4,1,1024]{2,1,0:T(1,128)S(1)}, bf16[2,128,1024]{2,1,0:T(8,...) custom-call(f32[128]{0:T(128)} %cot_hbm.1, ...), custom_call_target="tpu_custom_call" | custom-call | tf_op jit(solution)/shard_map/tile/pallas_call | solution.py:210
  21.2 0.5 %collective-permute-start.1 = (f32[4,1,1024]{2,1,0:T(1,128)S(1)}, f32[4,1,1024]{2,1,0:T(1,128)S(1)}, u32[]{:S(2)}, u32[]{:S(2)}) collective-permute-start(f32[4,1,1024]{2,1,0:T(1,128)S(1)} %get-tuple-element.23.lse_ref), channel_id=1, source_target_pairs={{0,1},{1,0},{2,3},{3,2},{4,5},{5,4},{6,7},{7,6},{8,9},{9,8},{10,11... | collective-permute-start | bytes 49160 | tf_op jit(solution)/shard_map/ppermute | solution.py:223
  21.7 0.1 collective-permute-start
  21.8 1.3 %even.1.gate_ref.even_ref = f32[2,128,1024]{2,1,0:T(8,128)S(1)} custom-call(bf16[4,2048,1024]{2,1,0:T(8,128)(2,1)S(1)} %get-tuple-element.18.e_ref, bf16[144,2048]{1,0:T(8,128)(2,1)S(1)} %get-tuple-element.22.dt_ref, f32[4,1,1024]{2,1,0:T(1,128)S(1)} %get-tuple-element.23.lse_ref, f32[4,1,1024]{2,1,0:T(1,128)S(1)} %get-tuple-element.20.top_ref), custom_call_target="tpu_custom_call" | custom-call | flops 8589934592 | bytes 1048576 | tf_op jit(solution)/shard_map/even/pallas_call | solution.py:210
  23.0 0.0 collective-permute-done.1.other_lse_ref
  23.1 4.1 %collective-permute-start.4 = (f32[4,1,1024]{2,1,0:T(1,128)S(1)}, f32[4,1,1024]{2,1,0:T(1,128)S(1)}, u32[]{:S(2)}, u32[]{:S(2)}) collective-permute-start(f32[4,1,1024]{2,1,0:T(1,128)S(1)} %pair.1.pair_ref), channel_id=1, source_target_pairs={{0,4},{1,5},{2,6},{3,7},{4,0},{5,1},{6,2},{7,3},{8,12},{9,13},{10,... | collective-permute-start | bytes 49160 | tf_op jit(solution)/shard_map/ppermute | solution.py:223
  27.1 1.4 %collective-permute-start.3 = (f32[4,1,1024]{2,1,0:T(1,128)S(1)}, f32[4,1,1024]{2,1,0:T(1,128)S(1)}, u32[]{:S(2)}, u32[]{:S(2)}) collective-permute-start(f32[4,1,1024]{2,1,0:T(1,128)S(1)} %pair.1.pair_ref), channel_id=1, source_target_pairs={{0,6},{1,7},{2,4},{3,5},{4,2},{5,3},{6,0},{7,1},{8,14},{9,15},{10,... | collective-permute-start | bytes 49160 | tf_op jit(solution)/shard_map/ppermute | solution.py:223
  28.5 0.2 collective-permute-start.2
  28.7 0.0 collective-permute-done.other_ref
  28.7 0.2 mean.1
  28.9 1.9 %collective-permute-start.5 = (bf16[128,512]{1,0:T(8,128)(2,1)S(1)}, bf16[128,512]{1,0:T(8,128)(2,1)S(1)}, u32[]{:S(2)}, u32[]{:S(2)}) collective-permute-start(bf16[128,512]{1,0:T(8,128)(2,1)S(1)} %get-tuple-element.27), channel_id=1, source_target_pairs={{0,2},{1,3},{2,0},{3,1},{4,6},{5,7},{6,4},{7,5},{8,10},{9,11},{10,... | collective-permute-start | bytes 393224 | tf_op jit(solution)/shard_map/ppermute | solution.py:223
  30.8 1.7 %collective-permute-start.6 = (bf16[128,512]{1,0:T(8,128)(2,1)S(1)}, bf16[128,512]{1,0:T(8,128)(2,1)S(1)}, u32[]{:S(2)}, u32[]{:S(2)}) collective-permute-start(bf16[128,512]{1,0:T(8,128)(2,1)S(1)} %get-tuple-element.28), channel_id=1, source_target_pairs={{0,4},{1,5},{2,6},{3,7},{4,0},{5,1},{6,2},{7,3},{8,12},{9,13},{10,... | collective-permute-start | bytes 393224 | tf_op jit(solution)/shard_map/ppermute | solution.py:223
  32.5 0.0 collective-permute-done.4.refs_2_
  32.5 0.9 %collective-permute-start.7 = (bf16[128,512]{1,0:T(8,128)(2,1)S(1)}, bf16[128,512]{1,0:T(8,128)(2,1)S(1)}, u32[]{:S(2)}, u32[]{:S(2)}) collective-permute-start(bf16[128,512]{1,0:T(8,128)(2,1)S(1)} %get-tuple-element.29), channel_id=1, source_target_pairs={{0,6},{1,7},{2,4},{3,5},{4,2},{5,3},{6,0},{7,1},{8,14},{9,15},{10,... | collective-permute-start | bytes 393224 | tf_op jit(solution)/shard_map/ppermute | solution.py:223
  33.4 0.0 collective-permute-done.3.refs_1_
  33.4 0.0 collective-permute-done.2.refs_0_
  33.4 3.5 %docs.1 = (f32[4,1,512]{2,1,0:T(1,128)S(1)}, bf16[4,256,1024]{2,1,0:T(8,128)(2,1)S(1)}, bf16[512,128]{1,0:T(8,128)(2,1)S(1)}, bf16[512,128]{1,0:T(8,128)(2,1)S(1)}, bf16[512,128]{1,0:T(8,128)(2,1)S(1)}) custom-call(bf16[4,2048,1024]{2,1,0:T(8,128)(2,1)S(1)} %get-tuple-element.18.e_ref, bf16[4,128,1024]{2,1,0:T(8,128)(2,1)S(1)} %get-tuple-element.19.qt_ref, ...), custom_call_target="tpu_custom_call" | custom-call | flops 42949672960 | bytes 1048576 | tf_op jit(solution)/shard_map/docs/pallas_call | solution.py:210
  36.9 2.5 %collective-permute-start.8 = (bf16[512,128]{1,0:T(8,128)(2,1)S(1)}, bf16[512,128]{1,0:T(8,128)(2,1)S(1)}, u32[]{:S(2)}, u32[]{:S(2)}) collective-permute-start(bf16[512,128]{1,0:T(8,128)(2,1)S(1)} %get-tuple-element.31), channel_id=1, source_target_pairs={{0,24},{8,16},{16,8},{24,0},{1,25},{9,17},{17,9},{25,1},{2,26},{10... | collective-permute-start | bytes 393224 | tf_op jit(solution)/shard_map/ppermute | solution.py:223
  39.4 0.5 %collective-permute-start.9 = (bf16[512,128]{1,0:T(8,128)(2,1)S(1)}, bf16[512,128]{1,0:T(8,128)(2,1)S(1)}, u32[]{:S(2)}, u32[]{:S(2)}) collective-permute-start(bf16[512,128]{1,0:T(8,128)(2,1)S(1)} %get-tuple-element.32), channel_id=1, source_target_pairs={{0,16},{8,24},{16,0},{24,8},{1,17},{9,25},{17,1},{25,9},{2,18},{10... | collective-permute-start | bytes 393224 | tf_op jit(solution)/shard_map/ppermute | solution.py:223
  39.9 0.0 collective-permute-done.5.refs_0_
  39.9 0.5 %collective-permute-start.10 = (bf16[512,128]{1,0:T(8,128)(2,1)S(1)}, bf16[512,128]{1,0:T(8,128)(2,1)S(1)}, u32[]{:S(2)}, u32[]{:S(2)}) collective-permute-start(bf16[512,128]{1,0:T(8,128)(2,1)S(1)} %get-tuple-element.33), channel_id=1, source_target_pairs={{0,8},{8,0},{16,24},{24,16},{1,9},{9,1},{17,25},{25,17},{2,10},{10... | collective-permute-start | bytes 393224 | tf_op jit(solution)/shard_map/ppermute | solution.py:223
  40.4 1.3 %own.1 = f32[512,128]{1,0:T(8,128)S(1)} custom-call(bf16[4,2048,1024]{2,1,0:T(8,128)(2,1)S(1)} %get-tuple-element.18.e_ref, bf16[4,256,1024]{2,1,0:T(8,128)(2,1)S(1)} %get-tuple-element.30.fq_ref), custom_call_target="tpu_custom_call" | custom-call | flops 1073741824 | bytes 1048576 | tf_op jit(solution)/shard_map/own/pallas_call | solution.py:210
  41.7 1.4 %collective-permute-done.6.refs_1_ = bf16[128,512]{1,0:T(8,128)(2,1)S(1)} collective-permute-done((bf16[128,512]{1,0:T(8,128)(2,1)S(1)}, bf16[128,512]{1,0:T(8,128)(2,1)S(1)}, u32[]{:S(2)}, u32[]{:S(2)}) %collective-permute-start.6) | collective-permute-done | bytes 131104 | tf_op jit(solution)/shard_map/ppermute | solution.py:223
  43.1 0.0 collective-permute-done.7.refs_2_
  43.1 0.9 %queries.1 = f32[512,128]{1,0:T(8,128)} custom-call(f32[4,1,512]{2,1,0:T(1,128)S(1)} %get-tuple-element.26.share_ref, f32[128,512]{1,0:T(8,128)S(1)} %get-tuple-element.25.gate_ref.own_ref, bf16[128,512]{1,0:T(8,128)(2,1)S(1)} %collective-permute-done.5.refs_0_, bf16[128,512]{1,0:T(8,128)(2,1)S(1)} %collective-permute-done.6.refs_1_, ...), custom_call_target="tpu_custom_call" | custom-call | tf_op jit(solution)/shard_map/queries/pallas_call | solution.py:210
  44.0 0.1 collective-permute-done.8
  44.1 0.8 %collective-permute-done.9 = bf16[512,128]{1,0:T(8,128)(2,1)S(1)} collective-permute-done((bf16[512,128]{1,0:T(8,128)(2,1)S(1)}, bf16[512,128]{1,0:T(8,128)(2,1)S(1)}, u32[]{:S(2)}, u32[]{:S(2)}) %collective-permute-start.9) | collective-permute-done | bytes 131104 | tf_op jit(solution)/shard_map/ppermute | solution.py:223
  44.9 0.0 collective-permute-done.10
  44.9 0.8 %add_bitcast_fusion = f32[1,512,128]{2,1,0:T(8,128)} fusion(bf16[512,128]{1,0:T(8,128)(2,1)S(1)} %collective-permute-done.10, bf16[512,128]{1,0:T(8,128)(2,1)S(1)} %collective-permute-done.9, f32[512,128]{1,0:T(8,128)S(1)} %own.1, bf16[512,128]{1,0:T(8,128)(2,1)S(1)} %collective-permute-done.8), kind=kLoop, calls=%fused_computation | loop fusion | flops 393216 | bytes 917504 | tf_op jit(solution)/shard_map/broadcast_in_dim | solution.py:297
  (1 shorter events, 0.0 us)
Async XLA Ops:
  21.2 1.9 %collective-permute-start.1 = (f32[4,1,1024]{2,1,0:T(1,128)S(1)}, f32[4,1,1024]{2,1,0:T(1,128)S(1)}, u32[]{:S(2)}, u32[]{:S(2)}) collective-permute-start(f32[4,1,1024]{2,1,0:T(1,128)S(1)} %get-tuple-element.23.lse_ref), channel_id=1, source_target_pairs={{0,1},{1,0},{2,3},{3,2},{4,5},{5,4},{6,7},{7,6},{8,9},{9,8},{10,11... | collective-permute-start | bytes 49160 | tf_op jit(solution)/shard_map/ppermute | solution.py:223
  21.7 7.1 %collective-permute-start = (bf16[2,128,1024]{2,1,0:T(8,128)(2,1)S(1)}, bf16[2,128,1024]{2,1,0:T(8,128)(2,1)S(1)}, u32[]{:S(2)}, u32[]{:S(2)}) collective-permute-start(bf16[2,128,1024]{2,1,0:T(8,128)(2,1)S(1)} %get-tuple-element.24), channel_id=1, source_target_pairs={{0,1},{1,0},{2,3},{3,2},{4,5},{5,4},{6,7},{7,6},{8,9},{9,8},{10,11... | collective-permute-start | bytes 1572872 | tf_op jit(solution)/shard_map/ppermute | solution.py:223
  23.1 9.4 %collective-permute-start.4 = (f32[4,1,1024]{2,1,0:T(1,128)S(1)}, f32[4,1,1024]{2,1,0:T(1,128)S(1)}, u32[]{:S(2)}, u32[]{:S(2)}) collective-permute-start(f32[4,1,1024]{2,1,0:T(1,128)S(1)} %pair.1.pair_ref), channel_id=1, source_target_pairs={{0,4},{1,5},{2,6},{3,7},{4,0},{5,1},{6,2},{7,3},{8,12},{9,13},{10,... | collective-permute-start | bytes 49160 | tf_op jit(solution)/shard_map/ppermute | solution.py:223
  27.1 6.2 %collective-permute-start.3 = (f32[4,1,1024]{2,1,0:T(1,128)S(1)}, f32[4,1,1024]{2,1,0:T(1,128)S(1)}, u32[]{:S(2)}, u32[]{:S(2)}) collective-permute-start(f32[4,1,1024]{2,1,0:T(1,128)S(1)} %pair.1.pair_ref), channel_id=1, source_target_pairs={{0,6},{1,7},{2,4},{3,5},{4,2},{5,3},{6,0},{7,1},{8,14},{9,15},{10,... | collective-permute-start | bytes 49160 | tf_op jit(solution)/shard_map/ppermute | solution.py:223
  28.5 4.9 %collective-permute-start.2 = (f32[4,1,1024]{2,1,0:T(1,128)S(1)}, f32[4,1,1024]{2,1,0:T(1,128)S(1)}, u32[]{:S(2)}, u32[]{:S(2)}) collective-permute-start(f32[4,1,1024]{2,1,0:T(1,128)S(1)} %pair.1.pair_ref), channel_id=1, source_target_pairs={{0,2},{1,3},{2,0},{3,1},{4,6},{5,7},{6,4},{7,5},{8,10},{9,11},{10,... | collective-permute-start | bytes 49160 | tf_op jit(solution)/shard_map/ppermute | solution.py:223
  28.9 11.0 %collective-permute-start.5 = (bf16[128,512]{1,0:T(8,128)(2,1)S(1)}, bf16[128,512]{1,0:T(8,128)(2,1)S(1)}, u32[]{:S(2)}, u32[]{:S(2)}) collective-permute-start(bf16[128,512]{1,0:T(8,128)(2,1)S(1)} %get-tuple-element.27), channel_id=1, source_target_pairs={{0,2},{1,3},{2,0},{3,1},{4,6},{5,7},{6,4},{7,5},{8,10},{9,11},{10,... | collective-permute-start | bytes 393224 | tf_op jit(solution)/shard_map/ppermute | solution.py:223
  30.8 12.4 %collective-permute-start.6 = (bf16[128,512]{1,0:T(8,128)(2,1)S(1)}, bf16[128,512]{1,0:T(8,128)(2,1)S(1)}, u32[]{:S(2)}, u32[]{:S(2)}) collective-permute-start(bf16[128,512]{1,0:T(8,128)(2,1)S(1)} %get-tuple-element.28), channel_id=1, source_target_pairs={{0,4},{1,5},{2,6},{3,7},{4,0},{5,1},{6,2},{7,3},{8,12},{9,13},{10,... | collective-permute-start | bytes 393224 | tf_op jit(solution)/shard_map/ppermute | solution.py:223
  32.5 10.7 %collective-permute-start.7 = (bf16[128,512]{1,0:T(8,128)(2,1)S(1)}, bf16[128,512]{1,0:T(8,128)(2,1)S(1)}, u32[]{:S(2)}, u32[]{:S(2)}) collective-permute-start(bf16[128,512]{1,0:T(8,128)(2,1)S(1)} %get-tuple-element.29), channel_id=1, source_target_pairs={{0,6},{1,7},{2,4},{3,5},{4,2},{5,3},{6,0},{7,1},{8,14},{9,15},{10,... | collective-permute-start | bytes 393224 | tf_op jit(solution)/shard_map/ppermute | solution.py:223
  36.9 7.2 %collective-permute-start.8 = (bf16[512,128]{1,0:T(8,128)(2,1)S(1)}, bf16[512,128]{1,0:T(8,128)(2,1)S(1)}, u32[]{:S(2)}, u32[]{:S(2)}) collective-permute-start(bf16[512,128]{1,0:T(8,128)(2,1)S(1)} %get-tuple-element.31), channel_id=1, source_target_pairs={{0,24},{8,16},{16,8},{24,0},{1,25},{9,17},{17,9},{25,1},{2,26},{10... | collective-permute-start | bytes 393224 | tf_op jit(solution)/shard_map/ppermute | solution.py:223
  39.4 5.5 %collective-permute-start.9 = (bf16[512,128]{1,0:T(8,128)(2,1)S(1)}, bf16[512,128]{1,0:T(8,128)(2,1)S(1)}, u32[]{:S(2)}, u32[]{:S(2)}) collective-permute-start(bf16[512,128]{1,0:T(8,128)(2,1)S(1)} %get-tuple-element.32), channel_id=1, source_target_pairs={{0,16},{8,24},{16,0},{24,8},{1,17},{9,25},{17,1},{25,9},{2,18},{10... | collective-permute-start | bytes 393224 | tf_op jit(solution)/shard_map/ppermute | solution.py:223
  39.9 5.0 %collective-permute-start.10 = (bf16[512,128]{1,0:T(8,128)(2,1)S(1)}, bf16[512,128]{1,0:T(8,128)(2,1)S(1)}, u32[]{:S(2)}, u32[]{:S(2)}) collective-permute-start(bf16[512,128]{1,0:T(8,128)(2,1)S(1)} %get-tuple-element.33), channel_id=1, source_target_pairs={{0,8},{8,0},{16,24},{24,16},{1,9},{9,1},{17,25},{25,17},{2,10},{10... | collective-permute-start | bytes 393224 | tf_op jit(solution)/shard_map/ppermute | solution.py:223

commit v6 on v5

--- a/solution.py
+++ b/solution.py
@@ -11,7 +11,7 @@
 SCALE = 2.0 * 1.4426950408889634
 ROOM = 30.0
 COLUMNS = 1024
-DOCS = 512
+DOCS = 1024
 SAMPLE = 128
 F32 = jnp.float32
 BF16 = jnp.bfloat16

time: 45.8 us -> 45.8 us (level)
  no operation moved by 1% of the time
where the time goes in v6:
time: 45.8 us; the launch traced here: 45.6 us
  Pallas kernels  27.6 us (60%)
  starting transfers between devices  14.3 us (31%)
  waiting for transfers between devices  2.33 us (5%)
  other arithmetic  0.77 us (2%)
  between operations  0.69 us (2%)
    pallas_call x7, Pallas kernels, call(): pl.pallas_call(kernel, out_shape=tuple(outs), in_specs=[pl.BlockSpec(memo...  27.6 us
    ppermute x11, starting transfers between devices, swap(): lax.ppermute(x, axis, [(i, i ^ step) for i in range(lax.axis_size(axis))])  14.3 us
    ppermute x11, waiting for transfers between devices, swap(): lax.ppermute(x, axis, [(i, i ^ step) for i in range(lax.axis_size(axis))])  2.33 us
  transfers between devices with their start and end apart: 11, of which 3 were waited for; matrix products, arithmetic and copies ran while one was open for 0% of the time, Pallas kernels for 16%

profile of v6, /device:TPU:0, one launch (start us, length us, event | category | flops | bytes accessed | tf_op | source)
XLA Modules:
  0.0 45.6 jit_solution(10829898910508142244)
XLA Ops:
  0.6 20.5 %tile.1 = (bf16[4,2048,1024]{2,1,0:T(8,128)(2,1)S(1)}, bf16[4,128,1024]{2,1,0:T(8,128)(2,1)S(1)}, f32[4,1,1024]{2,1,0:T(1,128)S(1)}, bf16[2,128,1024]{2,1,0:T(8,...) custom-call(f32[128]{0:T(128)} %cot_hbm.1, ...), custom_call_target="tpu_custom_call" | custom-call | tf_op jit(solution)/shard_map/tile/pallas_call | solution.py:210
  21.1 0.5 %collective-permute-start.1 = (f32[4,1,1024]{2,1,0:T(1,128)S(1)}, f32[4,1,1024]{2,1,0:T(1,128)S(1)}, u32[]{:S(2)}, u32[]{:S(2)}) collective-permute-start(f32[4,1,1024]{2,1,0:T(1,128)S(1)} %get-tuple-element.23.lse_ref), channel_id=1, source_target_pairs={{0,1},{1,0},{2,3},{3,2},{4,5},{5,4},{6,7},{7,6},{8,9},{9,8},{10,11... | collective-permute-start | bytes 49160 | tf_op jit(solution)/shard_map/ppermute | solution.py:223
  21.6 0.1 collective-permute-start
  21.7 1.3 %even.1.gate_ref.even_ref = f32[2,128,1024]{2,1,0:T(8,128)S(1)} custom-call(bf16[4,2048,1024]{2,1,0:T(8,128)(2,1)S(1)} %get-tuple-element.18.e_ref, bf16[144,2048]{1,0:T(8,128)(2,1)S(1)} %get-tuple-element.22.dt_ref, f32[4,1,1024]{2,1,0:T(1,128)S(1)} %get-tuple-element.23.lse_ref, f32[4,1,1024]{2,1,0:T(1,128)S(1)} %get-tuple-element.20.top_ref), custom_call_target="tpu_custom_call" | custom-call | flops 8589934592 | bytes 1048576 | tf_op jit(solution)/shard_map/even/pallas_call | solution.py:210
  23.0 0.0 collective-permute-done.1.other_lse_ref
  23.0 4.1 %collective-permute-start.4 = (f32[4,1,1024]{2,1,0:T(1,128)S(1)}, f32[4,1,1024]{2,1,0:T(1,128)S(1)}, u32[]{:S(2)}, u32[]{:S(2)}) collective-permute-start(f32[4,1,1024]{2,1,0:T(1,128)S(1)} %pair.1.pair_ref), channel_id=1, source_target_pairs={{0,4},{1,5},{2,6},{3,7},{4,0},{5,1},{6,2},{7,3},{8,12},{9,13},{10,... | collective-permute-start | bytes 49160 | tf_op jit(solution)/shard_map/ppermute | solution.py:223
  27.1 1.4 %collective-permute-start.3 = (f32[4,1,1024]{2,1,0:T(1,128)S(1)}, f32[4,1,1024]{2,1,0:T(1,128)S(1)}, u32[]{:S(2)}, u32[]{:S(2)}) collective-permute-start(f32[4,1,1024]{2,1,0:T(1,128)S(1)} %pair.1.pair_ref), channel_id=1, source_target_pairs={{0,6},{1,7},{2,4},{3,5},{4,2},{5,3},{6,0},{7,1},{8,14},{9,15},{10,... | collective-permute-start | bytes 49160 | tf_op jit(solution)/shard_map/ppermute | solution.py:223
  28.5 0.2 collective-permute-start.2
  28.7 0.0 collective-permute-done.other_ref
  28.7 0.2 mean.1
  28.9 1.9 %collective-permute-start.5 = (bf16[128,512]{1,0:T(8,128)(2,1)S(1)}, bf16[128,512]{1,0:T(8,128)(2,1)S(1)}, u32[]{:S(2)}, u32[]{:S(2)}) collective-permute-start(bf16[128,512]{1,0:T(8,128)(2,1)S(1)} %get-tuple-element.27), channel_id=1, source_target_pairs={{0,2},{1,3},{2,0},{3,1},{4,6},{5,7},{6,4},{7,5},{8,10},{9,11},{10,... | collective-permute-start | bytes 393224 | tf_op jit(solution)/shard_map/ppermute | solution.py:223
  30.7 1.7 %collective-permute-start.6 = (bf16[128,512]{1,0:T(8,128)(2,1)S(1)}, bf16[128,512]{1,0:T(8,128)(2,1)S(1)}, u32[]{:S(2)}, u32[]{:S(2)}) collective-permute-start(bf16[128,512]{1,0:T(8,128)(2,1)S(1)} %get-tuple-element.28), channel_id=1, source_target_pairs={{0,4},{1,5},{2,6},{3,7},{4,0},{5,1},{6,2},{7,3},{8,12},{9,13},{10,... | collective-permute-start | bytes 393224 | tf_op jit(solution)/shard_map/ppermute | solution.py:223
  32.4 0.0 collective-permute-done.4.refs_2_
  32.4 0.9 %collective-permute-start.7 = (bf16[128,512]{1,0:T(8,128)(2,1)S(1)}, bf16[128,512]{1,0:T(8,128)(2,1)S(1)}, u32[]{:S(2)}, u32[]{:S(2)}) collective-permute-start(bf16[128,512]{1,0:T(8,128)(2,1)S(1)} %get-tuple-element.29), channel_id=1, source_target_pairs={{0,6},{1,7},{2,4},{3,5},{4,2},{5,3},{6,0},{7,1},{8,14},{9,15},{10,... | collective-permute-start | bytes 393224 | tf_op jit(solution)/shard_map/ppermute | solution.py:223
  33.3 0.0 collective-permute-done.3.refs_1_
  33.3 0.0 collective-permute-done.2.refs_0_
  33.3 3.5 %docs.1 = (f32[4,1,512]{2,1,0:T(1,128)S(1)}, bf16[4,256,1024]{2,1,0:T(8,128)(2,1)S(1)}, bf16[512,128]{1,0:T(8,128)(2,1)S(1)}, bf16[512,128]{1,0:T(8,128)(2,1)S(1)}, bf16[512,128]{1,0:T(8,128)(2,1)S(1)}) custom-call(bf16[4,2048,1024]{2,1,0:T(8,128)(2,1)S(1)} %get-tuple-element.18.e_ref, bf16[4,128,1024]{2,1,0:T(8,128)(2,1)S(1)} %get-tuple-element.19.qt_ref, ...), custom_call_target="tpu_custom_call" | custom-call | flops 42949672960 | bytes 1048576 | tf_op jit(solution)/shard_map/docs/pallas_call | solution.py:210
  36.8 2.5 %collective-permute-start.8 = (bf16[512,128]{1,0:T(8,128)(2,1)S(1)}, bf16[512,128]{1,0:T(8,128)(2,1)S(1)}, u32[]{:S(2)}, u32[]{:S(2)}) collective-permute-start(bf16[512,128]{1,0:T(8,128)(2,1)S(1)} %get-tuple-element.31), channel_id=1, source_target_pairs={{0,24},{8,16},{16,8},{24,0},{1,25},{9,17},{17,9},{25,1},{2,26},{10... | collective-permute-start | bytes 393224 | tf_op jit(solution)/shard_map/ppermute | solution.py:223
  39.3 0.5 %collective-permute-start.9 = (bf16[512,128]{1,0:T(8,128)(2,1)S(1)}, bf16[512,128]{1,0:T(8,128)(2,1)S(1)}, u32[]{:S(2)}, u32[]{:S(2)}) collective-permute-start(bf16[512,128]{1,0:T(8,128)(2,1)S(1)} %get-tuple-element.32), channel_id=1, source_target_pairs={{0,16},{8,24},{16,0},{24,8},{1,17},{9,25},{17,1},{25,9},{2,18},{10... | collective-permute-start | bytes 393224 | tf_op jit(solution)/shard_map/ppermute | solution.py:223
  39.9 0.0 collective-permute-done.5.refs_0_
  39.9 0.5 %collective-permute-start.10 = (bf16[512,128]{1,0:T(8,128)(2,1)S(1)}, bf16[512,128]{1,0:T(8,128)(2,1)S(1)}, u32[]{:S(2)}, u32[]{:S(2)}) collective-permute-start(bf16[512,128]{1,0:T(8,128)(2,1)S(1)} %get-tuple-element.33), channel_id=1, source_target_pairs={{0,8},{8,0},{16,24},{24,16},{1,9},{9,1},{17,25},{25,17},{2,10},{10... | collective-permute-start | bytes 393224 | tf_op jit(solution)/shard_map/ppermute | solution.py:223
  40.4 1.3 %own.1 = f32[512,128]{1,0:T(8,128)S(1)} custom-call(bf16[4,2048,1024]{2,1,0:T(8,128)(2,1)S(1)} %get-tuple-element.18.e_ref, bf16[4,256,1024]{2,1,0:T(8,128)(2,1)S(1)} %get-tuple-element.30.fq_ref), custom_call_target="tpu_custom_call" | custom-call | flops 1073741824 | bytes 1048576 | tf_op jit(solution)/shard_map/own/pallas_call | solution.py:210
  41.7 1.4 %collective-permute-done.6.refs_1_ = bf16[128,512]{1,0:T(8,128)(2,1)S(1)} collective-permute-done((bf16[128,512]{1,0:T(8,128)(2,1)S(1)}, bf16[128,512]{1,0:T(8,128)(2,1)S(1)}, u32[]{:S(2)}, u32[]{:S(2)}) %collective-permute-start.6) | collective-permute-done | bytes 131104 | tf_op jit(solution)/shard_map/ppermute | solution.py:223
  43.1 0.0 collective-permute-done.7.refs_2_
  43.1 0.9 %queries.1 = f32[512,128]{1,0:T(8,128)} custom-call(f32[4,1,512]{2,1,0:T(1,128)S(1)} %get-tuple-element.26.share_ref, f32[128,512]{1,0:T(8,128)S(1)} %get-tuple-element.25.gate_ref.own_ref, bf16[128,512]{1,0:T(8,128)(2,1)S(1)} %collective-permute-done.5.refs_0_, bf16[128,512]{1,0:T(8,128)(2,1)S(1)} %collective-permute-done.6.refs_1_, ...), custom_call_target="tpu_custom_call" | custom-call | tf_op jit(solution)/shard_map/queries/pallas_call | solution.py:210
  43.9 0.1 collective-permute-done.8
  44.0 0.8 %collective-permute-done.9 = bf16[512,128]{1,0:T(8,128)(2,1)S(1)} collective-permute-done((bf16[512,128]{1,0:T(8,128)(2,1)S(1)}, bf16[512,128]{1,0:T(8,128)(2,1)S(1)}, u32[]{:S(2)}, u32[]{:S(2)}) %collective-permute-start.9) | collective-permute-done | bytes 131104 | tf_op jit(solution)/shard_map/ppermute | solution.py:223
  44.9 0.0 collective-permute-done.10
  44.9 0.8 %add_bitcast_fusion = f32[1,512,128]{2,1,0:T(8,128)} fusion(bf16[512,128]{1,0:T(8,128)(2,1)S(1)} %collective-permute-done.10, bf16[512,128]{1,0:T(8,128)(2,1)S(1)} %collective-permute-done.9, f32[512,128]{1,0:T(8,128)S(1)} %own.1, bf16[512,128]{1,0:T(8,128)(2,1)S(1)} %collective-permute-done.8), kind=kLoop, calls=%fused_computation | loop fusion | flops 393216 | bytes 917504 | tf_op jit(solution)/shard_map/broadcast_in_dim | solution.py:297
  (1 shorter events, 0.0 us)
Async XLA Ops:
  21.1 1.9 %collective-permute-start.1 = (f32[4,1,1024]{2,1,0:T(1,128)S(1)}, f32[4,1,1024]{2,1,0:T(1,128)S(1)}, u32[]{:S(2)}, u32[]{:S(2)}) collective-permute-start(f32[4,1,1024]{2,1,0:T(1,128)S(1)} %get-tuple-element.23.lse_ref), channel_id=1, source_target_pairs={{0,1},{1,0},{2,3},{3,2},{4,5},{5,4},{6,7},{7,6},{8,9},{9,8},{10,11... | collective-permute-start | bytes 49160 | tf_op jit(solution)/shard_map/ppermute | solution.py:223
  21.6 7.1 %collective-permute-start = (bf16[2,128,1024]{2,1,0:T(8,128)(2,1)S(1)}, bf16[2,128,1024]{2,1,0:T(8,128)(2,1)S(1)}, u32[]{:S(2)}, u32[]{:S(2)}) collective-permute-start(bf16[2,128,1024]{2,1,0:T(8,128)(2,1)S(1)} %get-tuple-element.24), channel_id=1, source_target_pairs={{0,1},{1,0},{2,3},{3,2},{4,5},{5,4},{6,7},{7,6},{8,9},{9,8},{10,11... | collective-permute-start | bytes 1572872 | tf_op jit(solution)/shard_map/ppermute | solution.py:223
  23.0 9.4 %collective-permute-start.4 = (f32[4,1,1024]{2,1,0:T(1,128)S(1)}, f32[4,1,1024]{2,1,0:T(1,128)S(1)}, u32[]{:S(2)}, u32[]{:S(2)}) collective-permute-start(f32[4,1,1024]{2,1,0:T(1,128)S(1)} %pair.1.pair_ref), channel_id=1, source_target_pairs={{0,4},{1,5},{2,6},{3,7},{4,0},{5,1},{6,2},{7,3},{8,12},{9,13},{10,... | collective-permute-start | bytes 49160 | tf_op jit(solution)/shard_map/ppermute | solution.py:223
  27.1 6.2 %collective-permute-start.3 = (f32[4,1,1024]{2,1,0:T(1,128)S(1)}, f32[4,1,1024]{2,1,0:T(1,128)S(1)}, u32[]{:S(2)}, u32[]{:S(2)}) collective-permute-start(f32[4,1,1024]{2,1,0:T(1,128)S(1)} %pair.1.pair_ref), channel_id=1, source_target_pairs={{0,6},{1,7},{2,4},{3,5},{4,2},{5,3},{6,0},{7,1},{8,14},{9,15},{10,... | collective-permute-start | bytes 49160 | tf_op jit(solution)/shard_map/ppermute | solution.py:223
  28.5 4.9 %collective-permute-start.2 = (f32[4,1,1024]{2,1,0:T(1,128)S(1)}, f32[4,1,1024]{2,1,0:T(1,128)S(1)}, u32[]{:S(2)}, u32[]{:S(2)}) collective-permute-start(f32[4,1,1024]{2,1,0:T(1,128)S(1)} %pair.1.pair_ref), channel_id=1, source_target_pairs={{0,2},{1,3},{2,0},{3,1},{4,6},{5,7},{6,4},{7,5},{8,10},{9,11},{10,... | collective-permute-start | bytes 49160 | tf_op jit(solution)/shard_map/ppermute | solution.py:223
  28.9 11.0 %collective-permute-start.5 = (bf16[128,512]{1,0:T(8,128)(2,1)S(1)}, bf16[128,512]{1,0:T(8,128)(2,1)S(1)}, u32[]{:S(2)}, u32[]{:S(2)}) collective-permute-start(bf16[128,512]{1,0:T(8,128)(2,1)S(1)} %get-tuple-element.27), channel_id=1, source_target_pairs={{0,2},{1,3},{2,0},{3,1},{4,6},{5,7},{6,4},{7,5},{8,10},{9,11},{10,... | collective-permute-start | bytes 393224 | tf_op jit(solution)/shard_map/ppermute | solution.py:223
  30.7 12.4 %collective-permute-start.6 = (bf16[128,512]{1,0:T(8,128)(2,1)S(1)}, bf16[128,512]{1,0:T(8,128)(2,1)S(1)}, u32[]{:S(2)}, u32[]{:S(2)}) collective-permute-start(bf16[128,512]{1,0:T(8,128)(2,1)S(1)} %get-tuple-element.28), channel_id=1, source_target_pairs={{0,4},{1,5},{2,6},{3,7},{4,0},{5,1},{6,2},{7,3},{8,12},{9,13},{10,... | collective-permute-start | bytes 393224 | tf_op jit(solution)/shard_map/ppermute | solution.py:223
  32.4 10.7 %collective-permute-start.7 = (bf16[128,512]{1,0:T(8,128)(2,1)S(1)}, bf16[128,512]{1,0:T(8,128)(2,1)S(1)}, u32[]{:S(2)}, u32[]{:S(2)}) collective-permute-start(bf16[128,512]{1,0:T(8,128)(2,1)S(1)} %get-tuple-element.29), channel_id=1, source_target_pairs={{0,6},{1,7},{2,4},{3,5},{4,2},{5,3},{6,0},{7,1},{8,14},{9,15},{10,... | collective-permute-start | bytes 393224 | tf_op jit(solution)/shard_map/ppermute | solution.py:223
  36.8 7.2 %collective-permute-start.8 = (bf16[512,128]{1,0:T(8,128)(2,1)S(1)}, bf16[512,128]{1,0:T(8,128)(2,1)S(1)}, u32[]{:S(2)}, u32[]{:S(2)}) collective-permute-start(bf16[512,128]{1,0:T(8,128)(2,1)S(1)} %get-tuple-element.31), channel_id=1, source_target_pairs={{0,24},{8,16},{16,8},{24,0},{1,25},{9,17},{17,9},{25,1},{2,26},{10... | collective-permute-start | bytes 393224 | tf_op jit(solution)/shard_map/ppermute | solution.py:223
  39.3 5.5 %collective-permute-start.9 = (bf16[512,128]{1,0:T(8,128)(2,1)S(1)}, bf16[512,128]{1,0:T(8,128)(2,1)S(1)}, u32[]{:S(2)}, u32[]{:S(2)}) collective-permute-start(bf16[512,128]{1,0:T(8,128)(2,1)S(1)} %get-tuple-element.32), channel_id=1, source_target_pairs={{0,16},{8,24},{16,0},{24,8},{1,17},{9,25},{17,1},{25,9},{2,18},{10... | collective-permute-start | bytes 393224 | tf_op jit(solution)/shard_map/ppermute | solution.py:223
  39.9 5.0 %collective-permute-start.10 = (bf16[512,128]{1,0:T(8,128)(2,1)S(1)}, bf16[512,128]{1,0:T(8,128)(2,1)S(1)}, u32[]{:S(2)}, u32[]{:S(2)}) collective-permute-start(bf16[512,128]{1,0:T(8,128)(2,1)S(1)} %get-tuple-element.33), channel_id=1, source_target_pairs={{0,8},{8,0},{16,24},{24,16},{1,9},{9,1},{17,25},{25,17},{2,10},{10... | collective-permute-start | bytes 393224 | tf_op jit(solution)/shard_map/ppermute | solution.py:223
